TPU v7x, 128 devices: a whole 4x4x4 slice. The times are simulated.
128 devices in a mesh: rep: 16 (over y, x_lo, core), shard: 8 (over x_hi, z).
Axes of the slice: x: 4 (x_hi: 2, x_lo: 2; x = x_hi * 2 + x_lo), y: 4, z: 4, core: 2. Of those that a mesh axis runs over, the one named last changes fastest.
Arguments:
- tokens: bfloat16 [32768, 1024], P(('rep', 'shard')), may hold values from -6 to 6
- out_grad: bfloat16 [32768, 1024], P(('rep', 'shard')), may hold values from -6 to 6
- segments: int32 [32768], P(('rep', 'shard')), may hold values from 0 to 4, as said below
- w_qkv: float32 [1024, 3072], P('shard'), may hold values from -0.1875 to 0.1875
- w_proj: float32 [1024, 1024], P('shard'), may hold values from -0.5 to 0.5
- w_up: float32 [1024, 4096], P('shard'), may hold values from -0.1875 to 0.1875
- w_down: float32 [1024, 4096], P('shard'), may hold values from -0.09375 to 0.09375
- norm_params: float32 [4, 1024], P(None, 'shard'), may hold values from -1 to 1.4
- biases: float32 [9216], P('shard'), may hold values from -1.5 to 1.5
- prior_moment_qkv: float32 [1024, 3072], P('shard'), may hold values from -64 to 64
- prior_square_qkv: float32 [1024, 3072], P('shard'), may hold values from 425.984 to 1736.704
- prior_moment_proj: float32 [1024, 1024], P('shard'), may hold values from -24 to 24
- prior_square_proj: float32 [1024, 1024], P('shard'), may hold values from 68.8128 to 275.2512
- prior_moment_up: float32 [1024, 4096], P('shard'), may hold values from -32 to 32
- prior_square_up: float32 [1024, 4096], P('shard'), may hold values from 157.2864 to 622.592
- prior_moment_down: float32 [1024, 4096], P('shard'), may hold values from -64 to 64
- prior_square_down: float32 [1024, 4096], P('shard'), may hold values from 622.592 to 2490.368
- prior_moment_norm: float32 [4, 1024], P(None, 'shard'), may hold values from -64 to 64
- prior_square_norm: float32 [4, 1024], P(None, 'shard'), may hold values from 425.984 to 1736.704
- prior_moment_bias: float32 [9216], P('shard'), may hold values from -64 to 64
- prior_square_bias: float32 [9216], P('shard'), may hold values from 425.984 to 1736.704
Outputs:
- block_out: bfloat16 [32768, 1024], P(('rep', 'shard'))
- grad_tokens: float32 [32768, 1024], P(('rep', 'shard'))
- updated_qkv: float32 [1024, 3072], P('shard')
- moment_qkv: float32 [1024, 3072], P('shard')
- square_qkv: float32 [1024, 3072], P('shard')
- updated_proj: float32 [1024, 1024], P('shard')
- moment_proj: float32 [1024, 1024], P('shard')
- square_proj: float32 [1024, 1024], P('shard')
- updated_up: float32 [1024, 4096], P('shard')
- moment_up: float32 [1024, 4096], P('shard')
- square_up: float32 [1024, 4096], P('shard')
- updated_down: float32 [1024, 4096], P('shard')
- moment_down: float32 [1024, 4096], P('shard')
- square_down: float32 [1024, 4096], P('shard')
- updated_norm: float32 [4, 1024], P(None, 'shard')
- moment_norm: float32 [4, 1024], P(None, 'shard')
- square_norm: float32 [4, 1024], P(None, 'shard')
- updated_bias: float32 [9216], P('shard')
- moment_bias: float32 [9216], P('shard')
- square_bias: float32 [9216], P('shard')
Inputs may be any that keep to these rules, and one draw needn't show every extreme that they name: `segments`: within each sequence of 2048 tokens the numbers never fall and run 0, 1, 2, 3, 4: five documents; the first two together, and the last two together, hold 64 to 128 tokens.
All inputs are finite; a program needn't handle non-finite values.
Results may differ from a plain program's by a relative error of at most 0.012.
Values may be sent and summed in bfloat16 or wider, within the bound.
No kernel may reach another device: no remote copies, remote signals or barrier semaphores. Data moves between devices by JAX's collectives and lax.ppermute only.
A program may use at most 320 MiB of HBM per device.

v0:
```python
import jax
import jax.numpy as jnp
from jax import lax
from jax.sharding import PartitionSpec as P

HEAD_DIM = 64
ROT = 16
STEP = 10


EPS_NORM = 1e-05
BETA_ONE = 0.9
BETA_TWO = 0.95
RATE_MATRIX = 0.05
RATE_VECTOR = 0.3
DECAY = 0.01
ADAM_EPS = 1e-08
NEGATIVE = -1e30


def layer_norm(values, norm_gain, norm_shift):
    centred = values - jnp.mean(values, axis=-1, keepdims=True)
    spread = jnp.mean(centred * centred, axis=-1, keepdims=True)
    return centred * lax.rsqrt(spread + EPS_NORM) * norm_gain + norm_shift


def gelu_exact(values):
    return jax.nn.gelu(values, approximate=False)


def rotary_tables(positions):
    rot_half = ROT // 2
    frequency = 10000.0 ** (-2.0 * jnp.arange(rot_half, dtype=jnp.float32) / ROT)
    angles = positions.astype(jnp.float32)[:, None] * frequency[None, :]
    angles = jnp.concatenate([angles, angles], axis=-1)
    return (jnp.cos(angles), jnp.sin(angles))


def rotate(values, cosine, sine):
    rot_half = ROT // 2
    rot_head = values[..., :ROT]
    turned = jnp.concatenate([-rot_head[..., rot_half:], rot_head[..., :rot_half]], axis=-1)
    rotated = rot_head * cosine[:, None, :] + turned * sine[:, None, :]
    return jnp.concatenate([rotated, values[..., ROT:]], axis=-1)


def contract_rows(left, right):
    return lax.dot_general(
        left, right, (((0,), (0,)), ((), ())), preferred_element_type=jnp.float32
    )


def adam_step(weight, moment, square, gradient, rate, decay):
    moment_new = BETA_ONE * moment + (1.0 - BETA_ONE) * gradient
    square_new = BETA_TWO * square + (1.0 - BETA_TWO) * gradient * gradient
    fixed_moment = moment_new / (1.0 - BETA_ONE**STEP)
    fixed_square = square_new / (1.0 - BETA_TWO**STEP)
    weight_new = weight - rate * (
        fixed_moment / (jnp.sqrt(fixed_square) + ADAM_EPS) + decay * weight
    )
    return (weight_new, moment_new, square_new)


def body(
    tokens,
    out_grad,
    segments,
    w_qkv,
    w_proj,
    w_up,
    w_down,
    norm_params,
    biases,
    prior_moment_qkv,
    prior_square_qkv,
    prior_moment_proj,
    prior_square_proj,
    prior_moment_up,
    prior_square_up,
    prior_moment_down,
    prior_square_down,
    prior_moment_norm,
    prior_square_norm,
    prior_moment_bias,
    prior_square_bias,
):
    tok_rows = tokens.shape[0]
    model_width = tokens.shape[1]
    shard_index = lax.axis_index("shard")
    head_count = model_width // HEAD_DIM
    full_qkv, full_proj, full_up, full_down, full_norm, full_bias = (
        lax.all_gather(w_qkv.astype(jnp.bfloat16), "shard", axis=0, tiled=True),
        lax.all_gather(w_proj.astype(jnp.bfloat16), "shard", axis=0, tiled=True),
        lax.all_gather(w_up.astype(jnp.bfloat16), "shard", axis=0, tiled=True),
        lax.all_gather(w_down.astype(jnp.bfloat16), "shard", axis=0, tiled=True),
        lax.all_gather(norm_params.astype(jnp.bfloat16), "shard", axis=1, tiled=True),
        lax.all_gather(biases.astype(jnp.bfloat16), "shard", axis=0, tiled=True),
    )
    ffn_width = full_up.shape[1]
    norm_vals = full_norm.astype(jnp.float32)
    bias_vals = full_bias.astype(jnp.float32)
    bias_qkv = bias_vals[: 3 * model_width]
    bias_proj = bias_vals[3 * model_width : 4 * model_width]
    bias_up = bias_vals[4 * model_width : 4 * model_width + ffn_width]
    bias_down = bias_vals[4 * model_width + ffn_width :]
    all_docs = lax.all_gather(segments, "shard", axis=0, tiled=True)
    query_ids = shard_index * tok_rows + jnp.arange(tok_rows, dtype=jnp.int32)
    doc_start = jnp.sum((all_docs[None, :] < segments[:, None]).astype(jnp.int32), axis=1)
    cosine, sine = rotary_tables(query_ids - doc_start)
    inputs = tokens.astype(jnp.float32)
    normed_one, norm_back_one = jax.vjp(layer_norm, inputs, norm_vals[0], norm_vals[1])
    normed_one = normed_one.astype(jnp.bfloat16)
    qkv_vals = jnp.dot(normed_one, full_qkv, preferred_element_type=jnp.float32) + bias_qkv
    queries = rotate(
        qkv_vals[:, :model_width].reshape(tok_rows, head_count, HEAD_DIM), cosine, sine
    )
    queries = queries.astype(jnp.bfloat16)
    key_flat = rotate(
        qkv_vals[:, model_width : 2 * model_width].reshape(tok_rows, head_count, HEAD_DIM),
        cosine,
        sine,
    )
    key_flat = key_flat.astype(jnp.bfloat16).reshape(tok_rows, model_width)
    value_flat = qkv_vals[:, 2 * model_width :].astype(jnp.bfloat16)

    def piece_scores(key_block):
        piece_rows = key_block.shape[0]
        scores = (
            jnp.einsum("qhd,khd->hqk", queries, key_block, preferred_element_type=jnp.float32)
            * 0.125
        )
        key_ids = jnp.arange(piece_rows, dtype=jnp.int32)
        allowed = (key_ids[None, :] <= query_ids[:, None]) & (
            all_docs[None, :] == segments[:, None]
        )
        return (scores, allowed)

    pieces = (
        lax.all_gather(key_flat, "shard", axis=0, tiled=True),
        lax.all_gather(value_flat, "shard", axis=0, tiled=True),
    )
    run_max = jnp.full((head_count, tok_rows), NEGATIVE, jnp.float32)
    numer = jnp.zeros((tok_rows, head_count, HEAD_DIM), jnp.float32)
    piece_rows = pieces[0].shape[0]
    key_block = pieces[0].reshape(piece_rows, head_count, HEAD_DIM)
    value_block = pieces[1].reshape(piece_rows, head_count, HEAD_DIM)
    scores, allowed = piece_scores(key_block)
    new_max = jnp.maximum(run_max, jnp.max(jnp.where(allowed[None], scores, NEGATIVE), axis=-1))
    expo_vals = jnp.where(allowed[None], jnp.exp(scores - new_max[..., None]), 0.0)
    fade = jnp.exp(run_max - new_max)
    run_sum = jnp.sum(expo_vals, axis=-1)
    numer = numer * fade.T[:, :, None] + jnp.einsum(
        "hqk,khd->qhd",
        expo_vals.astype(jnp.bfloat16),
        value_block,
        preferred_element_type=jnp.float32,
    )
    row_max, row_sum, numer = (new_max, run_sum, numer)
    context = numer / row_sum.T[:, :, None]
    context_low = context.reshape(tok_rows, model_width).astype(jnp.bfloat16)
    attn_out = jnp.dot(context_low, full_proj, preferred_element_type=jnp.float32) + bias_proj
    normed_two, norm_back_two = jax.vjp(layer_norm, inputs, norm_vals[2], norm_vals[3])
    normed_two = normed_two.astype(jnp.bfloat16)
    pre_act = jnp.dot(normed_two, full_up, preferred_element_type=jnp.float32) + bias_up
    hidden, gelu_back = jax.vjp(gelu_exact, pre_act)
    hidden_low = hidden.astype(jnp.bfloat16)
    down_out = (
        jnp.einsum("tf,df->td", hidden_low, full_down, preferred_element_type=jnp.float32)
        + bias_down
    )
    block_out = (inputs + attn_out + down_out).astype(jnp.bfloat16)
    grad_context = jnp.einsum("td,ed->te", out_grad, full_proj, preferred_element_type=jnp.float32)
    grad_context = grad_context.reshape(tok_rows, head_count, HEAD_DIM)
    grad_merged = (grad_context / row_sum.T[:, :, None]).astype(jnp.bfloat16)
    centre = jnp.sum(grad_context * context, axis=-1).T / row_sum
    pieces = (
        lax.all_gather(key_flat, "shard", axis=0, tiled=True),
        lax.all_gather(value_flat, "shard", axis=0, tiled=True),
    )
    piece_rows = pieces[0].shape[0]
    piece_piece_rows = pieces[0].shape[0]
    key_block = pieces[0].reshape(piece_piece_rows, head_count, HEAD_DIM)
    value_block = pieces[1].reshape(piece_piece_rows, head_count, HEAD_DIM)
    scores, allowed = piece_scores(key_block)
    expo_vals = jnp.where(allowed[None], jnp.exp(scores - row_max[..., None]), 0.0)
    grad_expo = jnp.einsum(
        "qhd,khd->hqk", grad_merged, value_block, preferred_element_type=jnp.float32
    )
    grad_scores = (expo_vals * (grad_expo - centre[..., None])).astype(jnp.bfloat16)
    key_block, expo_vals, grad_scores = (key_block, expo_vals, grad_scores)
    grad_query = jnp.einsum(
        "hqk,khd->qhd", grad_scores, key_block, preferred_element_type=jnp.float32
    )
    grad_key_block = (
        jnp.einsum("hqk,qhd->khd", grad_scores, queries, preferred_element_type=jnp.float32) * 0.125
    )
    grad_value_block = jnp.einsum(
        "hqk,qhd->khd",
        expo_vals.astype(jnp.bfloat16),
        grad_merged,
        preferred_element_type=jnp.float32,
    )
    term = jnp.concatenate(
        [
            grad_key_block.reshape(piece_rows, model_width),
            grad_value_block.reshape(piece_rows, model_width),
        ],
        axis=1,
    )
    key_terms = term
    fold_result = (grad_query, key_terms)
    query_grads, key_terms = fold_result
    key_grads = lax.psum_scatter(key_terms, "shard", scatter_dimension=0, tiled=True)
    grad_queries = rotate(query_grads * 0.125, cosine, -sine).reshape(tok_rows, model_width)
    grad_keys = rotate(
        key_grads[:, :model_width].reshape(tok_rows, head_count, HEAD_DIM), cosine, -sine
    )
    grad_qkv = jnp.concatenate(
        [grad_queries, grad_keys.reshape(tok_rows, model_width), key_grads[:, model_width:]], axis=1
    ).astype(jnp.bfloat16)
    grad_hidden = jnp.dot(out_grad, full_down, preferred_element_type=jnp.float32)
    grad_pre = gelu_back(grad_hidden)[0].astype(jnp.bfloat16)
    grad_normed_one = jnp.einsum(
        "tc,dc->td", grad_qkv, full_qkv, preferred_element_type=jnp.float32
    )
    grad_normed_two = jnp.einsum("tf,df->td", grad_pre, full_up, preferred_element_type=jnp.float32)
    back_one = norm_back_one(grad_normed_one)
    back_two = norm_back_two(grad_normed_two)
    grad_tokens = out_grad.astype(jnp.float32) + back_one[0] + back_two[0]
    norm_grad = jnp.stack([back_one[1], back_one[2], back_two[1], back_two[2]], axis=0)
    out_colsum = jnp.sum(out_grad, axis=0, dtype=jnp.float32)
    bias_grad = jnp.concatenate(
        [
            jnp.sum(grad_qkv, axis=0, dtype=jnp.float32),
            out_colsum,
            jnp.sum(grad_pre, axis=0, dtype=jnp.float32),
            out_colsum,
        ],
        axis=0,
    )
    matrix_grad = lax.psum_scatter(
        jnp.concatenate(
            [
                contract_rows(normed_one, grad_qkv),
                contract_rows(context_low, out_grad),
                contract_rows(normed_two, grad_pre),
                contract_rows(out_grad, hidden_low),
            ],
            axis=1,
        ),
        "shard",
        scatter_dimension=0,
        tiled=True,
    )
    norm_part, bias_part = (
        lax.psum_scatter(norm_grad, "shard", scatter_dimension=1, tiled=True),
        lax.psum_scatter(bias_grad, "shard", scatter_dimension=0, tiled=True),
    )
    matrix_grad, norm_part, bias_part = lax.psum((matrix_grad, norm_part, bias_part), "rep")
    grad_w_qkv = matrix_grad[:, : 3 * model_width]
    grad_w_proj = matrix_grad[:, 3 * model_width : 4 * model_width]
    grad_w_up = matrix_grad[:, 4 * model_width : 4 * model_width + ffn_width]
    grad_w_down = matrix_grad[:, 4 * model_width + ffn_width :]
    new_qkv = adam_step(w_qkv, prior_moment_qkv, prior_square_qkv, grad_w_qkv, RATE_MATRIX, DECAY)
    new_proj = adam_step(
        w_proj, prior_moment_proj, prior_square_proj, grad_w_proj, RATE_MATRIX, DECAY
    )
    new_up = adam_step(w_up, prior_moment_up, prior_square_up, grad_w_up, RATE_MATRIX, DECAY)
    new_down = adam_step(
        w_down, prior_moment_down, prior_square_down, grad_w_down, RATE_MATRIX, DECAY
    )
    new_norm = adam_step(
        norm_params, prior_moment_norm, prior_square_norm, norm_part, RATE_VECTOR, 0.0
    )
    new_bias = adam_step(biases, prior_moment_bias, prior_square_bias, bias_part, RATE_VECTOR, 0.0)
    return (
        block_out,
        grad_tokens,
        new_qkv[0],
        new_qkv[1],
        new_qkv[2],
        new_proj[0],
        new_proj[1],
        new_proj[2],
        new_up[0],
        new_up[1],
        new_up[2],
        new_down[0],
        new_down[1],
        new_down[2],
        new_norm[0],
        new_norm[1],
        new_norm[2],
        new_bias[0],
        new_bias[1],
        new_bias[2],
    )


def solution(mesh):
    in_specs = (
        P(("rep", "shard"), None),
        P(("rep", "shard"), None),
        P(("rep", "shard")),
        P("shard", None),
        P("shard", None),
        P("shard", None),
        P("shard", None),
        P(None, "shard"),
        P("shard"),
        P("shard", None),
        P("shard", None),
        P("shard", None),
        P("shard", None),
        P("shard", None),
        P("shard", None),
        P("shard", None),
        P("shard", None),
        P(None, "shard"),
        P(None, "shard"),
        P("shard"),
        P("shard"),
    )
    out_specs = (
        P(("rep", "shard"), None),
        P(("rep", "shard"), None),
        P("shard", None),
        P("shard", None),
        P("shard", None),
        P("shard", None),
        P("shard", None),
        P("shard", None),
        P("shard", None),
        P("shard", None),
        P("shard", None),
        P("shard", None),
        P("shard", None),
        P("shard", None),
        P(None, "shard"),
        P(None, "shard"),
        P(None, "shard"),
        P("shard"),
        P("shard"),
        P("shard"),
    )
    return jax.shard_map(body, mesh=mesh, in_specs=in_specs, out_specs=out_specs, check_vma=False)
```

profile of v0, /device:TPU:1, one launch (start us, length us, event | category | flops | bytes accessed | tf_op | source)
XLA Modules:
  0.0 1495.4 jit_solution(15955745025627905065)
XLA Ops:
  7.3 2.4 convert_element_type.90
  9.8 1.8 convert_element_type.99
  11.7 30.0 %all-gather.1 = bf16[8,1,1152]{2,1,0:T(2,128)(2,1)S(1)} all-gather(bf16[1,1,1152]{2,1,0:T(2,128)(2,1)S(1)} %reshape.280), channel_id=1, replica_groups=mesh['rep'=16,'shard'=8] {'shard'}, dimensions={0}, use_global_device_ids=true | all-gather | bytes 20736 | tf_op jit(solution)/shard_map/all_gather | solution.py:97
  41.8 19.7 %all_gather.30 = bf16[4,1024]{1,0:T(4,128)(2,1)S(1)} all-gather(bf16[4,128]{1,0:T(4,128)(2,1)S(1)} %convert_element_type.87), channel_id=1, replica_groups=mesh['rep'=16,'shard'=8] {'shard'}, dimensions={1}, use_global_device_ids=true | all-gather | bytes 9216 | tf_op jit(solution)/shard_map/all_gather | solution.py:96
  61.9 41.0 %all-gather.9.cloned.1.call-done = bf16[1024,3072]{1,0:T(8,128)(2,1)} async-done(((bf16[128,3072]{1,0:T(8,128)(2,1)}), bf16[1024,3072]{1,0:T(8,128)(2,1)}) %all-gather.9.cloned.1.call-update) | async-done | bytes 6291472 | tf_op jit(solution)/shard_map/all_gather | solution.py:92
  103.0 4.7 convolution_add_fusion.1
  107.7 1.6 copy-done.23
  110.3 15.1 %all-gather = s32[8,1,256]{2,1,0:T(1,128)S(1)} all-gather(s32[1,1,256]{2,1,0:T(1,128)S(1)} %bitcast.124), channel_id=1, replica_groups=mesh['rep'=16,'shard'=8] {'shard'}, dimensions={0}, use_global_device_ids=true | all-gather | bytes 9216 | tf_op jit(solution)/shard_map/all_gather | solution.py:106
  126.5 3.1 fusion.78
  129.6 2.7 copy.62
  133.5 2.5 copy.61
  140.5 2.7 convert_element_type.103
  144.0 13.7 all-gather.15.cloned.1.call-done
  157.7 2.3 fusion.81
  161.2 68.8 %all-gather.13.cloned.1.call-done = bf16[2048,1024]{1,0:T(8,128)(2,1)} async-done(((bf16[256,1024]{1,0:T(8,128)(2,1)}), bf16[2048,1024]{1,0:T(8,128)(2,1)}) %all-gather.13.cloned.1.call-update) | async-done | bytes 4194320 | tf_op jit(solution)/shard_map/all_gather | solution.py:140
  230.0 6.5 copy.63
  236.5 67.8 %all-gather.11.cloned.1.call-done = bf16[2048,1024]{0,1:T(8,128)(2,1)} async-done(((bf16[256,1024]{0,1:T(8,128)(2,1)}), bf16[2048,1024]{0,1:T(8,128)(2,1)}) %all-gather.11.cloned.1.call-update) | async-done | bytes 4194320 | tf_op jit(solution)/shard_map/all_gather | solution.py:139
  304.3 16.8 %select_reduce_fusion = (f32[16,256]{1,0:T(8,128)S(1)}, f32[16,256,2048]{2,1,0:T(8,128)}) fusion(pred[256,2048]{1,0:T(8,128)(4,1)S(1)} %fusion.10, bf16[2048,16,64]{0,2,1:T(8,128)(2,1)} %bitcast.71, bf16[256,16,48]{0,2,1:T(8,128)(2,1)S(1)} %slice.222, bf16[256,16,16]{0,2,1:T(8,128)(2,1)S(1)} %get-tuple-element.77), kind=kOutput, calls=%fused_computation.3 | convolution fusion | flops 1099952128 | bytes 38813696 | tf_op jit(solution)/shard_map/qhd,khd->hqk/dot_general | solution.py:129
  321.1 15.3 %fusion = f32[16,256]{1,0:T(8,128)S(1)} fusion(f32[16,256,2048]{2,1,0:T(8,128)} %get-tuple-element.89, f32[16,256]{1,0:T(8,128)S(1)} %get-tuple-element.80, pred[256,2048]{1,0:T(8,128)(4,1)S(1)} %fusion.10), kind=kLoop, calls=%fused_computation.4 | loop fusion | flops 33550336 | bytes 34111488 | tf_op jit(solution)/shard_map/reduce_sum | solution.py:151
  336.5 16.5 %multiply_reduce_fusion = (f32[256,16]{0,1:T(8,128)S(1)}, bf16[256,16,64]{0,2,1:T(8,128)(2,1)}) fusion(f32[256,1024]{0,1:T(8,128)S(1)} %fusion.81, f32[256,16]{0,1:T(8,128)S(1)} %bitcast.116, bf16[2048,16,64]{0,2,1:T(8,128)(2,1)} %bitcast.80, f32[16,256,2048]{2,1,0:T(8,128)} %get-tuple-element.89, f32[16,256]{1,0:T(8,128)S(1)} %get-tuple-element.80, ...), kind=kOutput, calls=%fused_computation.84 | convolution fusion | flops 1108602880 | bytes 39911424 | tf_op jit(solution)/shard_map/hqk,khd->qhd/dot_general | solution.py:152
  353.0 23.1 %multiply_convert_fusion = bf16[16,256,2048]{2,1,0:T(8,128)(2,1)} fusion(bf16[2048,16,64]{0,2,1:T(8,128)(2,1)} %bitcast.81, f32[16,256,2048]{2,1,0:T(8,128)} %get-tuple-element.89, f32[16,256]{1,0:T(8,128)S(1)} %bitcast_divide_fusion, f32[16,256]{1,0:T(8,128)S(1)} %get-tuple-element.80, pred[256,2048]{1,0:T(8,128)(4,1)S(1)} %fusion.10, ...), kind=kOutput, calls=%fused_computation.1 | convolution fusion | flops 1124597760 | bytes 56147968 | tf_op jit(solution)/shard_map/qhd,khd->hqk/dot_general | solution.py:186
  376.1 12.0 convolution_multiply_fusion
  388.1 17.0 %fusion.47 = f32[16,64,2048]{2,1,0:T(8,128)} fusion(f32[16,256,2048]{2,1,0:T(8,128)} %get-tuple-element.89, f32[16,256]{1,0:T(8,128)S(1)} %get-tuple-element.80, pred[256,2048]{1,0:T(8,128)(4,1)S(1)} %fusion.10, f32[256,16,64]{0,2,1:T(8,128)S(1)} %bitcast.96, f32[256,16]{0,1:T(8,128)S(1)} %bitcast.118), kind=kOutput, calls=%fused_computation.115 | convolution fusion | flops 1107820544 | bytes 43548672 | tf_op jit(solution)/shard_map/hqk,qhd->khd/dot_general | solution.py:197
  405.1 11.6 pad_maximum_fusion.1
  416.9 7.8 convolution_add_fusion
  424.7 95.3 %all-gather.19.cloned.1.call-done = bf16[1024,4096]{1,0:T(8,128)(2,1)} async-done(((bf16[128,4096]{1,0:T(8,128)(2,1)}), bf16[1024,4096]{1,0:T(8,128)(2,1)}) %all-gather.19.cloned.1.call-update) | async-done | bytes 8388624 | tf_op jit(solution)/shard_map/all_gather | solution.py:95
  520.0 15.2 %convert_reduce_fusion = (f32[4096]{0:T(1024)}, bf16[256,4096]{1,0:T(8,128)(2,1)S(1)}, f32[256,4096]{1,0:T(8,128)S(1)}) fusion(f32[256,4096]{1,0:T(8,128)} %convolution_add_fusion, bf16[256,1024]{1,0:T(8,128)(2,1)S(1)} %copy-done.5, bf16[1024,4096]{1,0:T(8,128)(2,1)} %all-gather.19.cloned.1.call-done), kind=kOutput, calls=%fused_computation.12 | convolution fusion | flops 2225074176 | bytes 19415040 | tf_op jit(solution)/shard_map/dot_general | solution.py:221
  535.9 8.1 convolution_bitcast_fusion
  544.1 8.5 fusion.62
  552.5 14.2 fusion.22
  567.9 1.7 slice_negate_fusion.1
  569.6 3.7 fusion.83
  573.4 138.6 %reduce-scatter.6.cloned.1.call-done = f32[256,2048]{0,1:T(8,128)} async-done(((f32[2048,2048]{0,1:T(8,128)}), f32[256,2048]{0,1:T(8,128)}) %reduce-scatter.6.cloned.1.call-update) | async-done | bytes 2097168 | tf_op jit(solution)/shard_map/reduce_scatter | solution.py:213
  714.7 1.6 slice.217
  717.1 6.8 fusion.65
  724.0 33.2 %pad_maximum_fusion = f32[1024,12288]{1,0:T(8,128)} fusion(f32[1024,4096]{1,0:T(8,128)} %convolution_bitcast_fusion, f32[1024,4096]{1,0:T(8,128)} %fusion.62, f32[1024,1024]{1,0:T(8,128)} %fusion.83, f32[1024,3072]{1,0:T(8,128)} %fusion.65), kind=kLoop, calls=%fused_computation | loop fusion | flops 37748736 | bytes 100663296 | tf_op jit(solution)/shard_map/concatenate | solution.py:242
  757.3 6.5 fusion.82
  763.8 5.3 fusion.35
  771.3 470.1 %reduce-scatter.8.cloned.1.call-done = f32[128,12288]{1,0:T(8,128)} async-done(((f32[1024,12288]{1,0:T(8,128)}), f32[128,12288]{1,0:T(8,128)}) %reduce-scatter.8.cloned.1.call-update) | async-done | bytes 6291472 | tf_op jit(solution)/shard_map/reduce_scatter | solution.py:241
  1243.4 5.9 convolution_add_fusion.3
  1251.6 1.7 convert_reduce_fusion.4
  1253.3 33.4 %all-reduce = f32[9216]{0:T(1024)S(1)} all-reduce(f32[9216]{0:T(1024)S(1)} %pad_maximum_fusion.9), channel_id=5, replica_groups=mesh['rep'=16,'shard'=8] {'shard'}, use_global_device_ids=true, to_apply=%region_22.23.clone | all-reduce | flops 9216 | bytes 73728
  1286.8 28.5 %reduce-scatter.10.cloned.1.call-done = f32[128,4]{1,0:T(8,128)} async-done(((f32[1024,4]{1,0:T(8,128)}), f32[128,4]{1,0:T(8,128)}) %reduce-scatter.10.cloned.1.call-update) | async-done | bytes 2064
  1316.2 53.4 %all-reduce.1 = (f32[4,128]{1,0:T(4,128)S(1)}, f32[1152]{0:T(1024)S(1)}) all-reduce(f32[4,128]{1,0:T(4,128)S(1)} %copy.71, f32[1152]{0:T(1024)S(1)} %dynamic-slice.1), channel_id=1, replica_groups=mesh['rep'=16,'shard'=8] {'rep'}, use_global_device_ids=true, to_apply=%region_18.19 | all-reduce | flops 1664 | bytes 13312 | tf_op jit(solution)/shard_map/psum | solution.py:259
  1370.8 101.2 %all-reduce.4.cloned.1.call-done = f32[128,12288]{1,0:T(8,128)} async-done(((f32[128,12288]{1,0:T(8,128)}), f32[128,12288]{1,0:T(8,128)}) %all-reduce.4.cloned.1.call-update) | async-done | bytes 6291472 | tf_op jit(solution)/shard_map/psum | solution.py:259
  1472.0 5.6 multiply_subtract_fusion.2
  1477.6 3.4 multiply_subtract_fusion.3
  1481.1 7.2 multiply_subtract_fusion
  (171 shorter events, 23.7 us)
Async XLA Ops:
  7.2 4.5 copy-start.37
  7.2 34.5 %copy-start.45 = (f32[4,128]{1,0:T(4,128)S(1)}, f32[4,128]{1,0:T(4,128)}, u32[]{:S(2)}) copy-start(f32[4,128]{1,0:T(4,128)} %param.28) | copy-start | bytes 6148
  7.2 54.2 %copy-start = (bf16[256,1024]{1,0:T(8,128)(2,1)S(1)}, bf16[256,1024]{1,0:T(8,128)(2,1)}, u32[]{:S(2)}) copy-start(bf16[256,1024]{1,0:T(8,128)(2,1)} %param.21) | copy-start | bytes 1572868
  7.2 95.8 %all-gather.9.cloned.1.call-start = ((), (), s32[]{:S(2)}) async-start(), calls=%async_computation.3 | async-start | bytes 7077888 | tf_op jit(solution)/shard_map/all_gather | solution.py:92
  9.7 148.0 %all-gather.15.cloned.1.call-start = ((), (), s32[]{:S(2)}) async-start(), calls=%async_computation.6 | async-start | bytes 2359296 | tf_op jit(solution)/shard_map/all_gather | solution.py:93
  11.6 218.4 %all-gather.13.cloned.1.call-start = ((), (), s32[]{:S(2)}) async-start(), calls=%async_computation.5 | async-start | bytes 4718592 | tf_op jit(solution)/shard_map/all_gather | solution.py:140
  41.7 375.1 %copy-start.33 = (f32[8,1,1152]{2,1,0:T(1,128)}, f32[8,1,1152]{2,1,0:T(1,128)S(1)}, u32[]{:S(2)}) copy-start(f32[8,1,1152]{2,1,0:T(1,128)S(1)} %convert_element_type.111) | copy-start | bytes 110596
  61.9 45.8 %copy-start.41 = (f32[256]{0:T(256)}, f32[256]{0:T(256)S(1)}, u32[]{:S(2)}) copy-start(f32[256]{0:T(256)S(1)} %fusion.34) | copy-start | bytes 3076
  61.9 482.2 %copy-start.34 = (f32[256]{0:T(256)}, f32[256]{0:T(256)S(1)}, u32[]{:S(2)}) copy-start(f32[256]{0:T(256)S(1)} %fusion.54) | copy-start | bytes 3076
  61.9 45.8 %copy-start.28 = (f32[1,1024]{1,0:T(1,128)}, f32[1,1024]{1,0:T(1,128)S(1)}, u32[]{:S(2)}) copy-start(f32[1,1024]{1,0:T(1,128)S(1)} %get-tuple-element.84) | copy-start | bytes 12292
  61.9 45.8 %copy-start.30 = (f32[1,1024]{1,0:T(1,128)}, f32[1,1024]{1,0:T(1,128)S(1)}, u32[]{:S(2)}) copy-start(f32[1,1024]{1,0:T(1,128)S(1)} %get-tuple-element.85) | copy-start | bytes 12292
  103.0 7.3 copy-start.40
  110.3 194.0 %all-gather.11.cloned.1.call-start = ((), (), s32[]{:S(2)}) async-start(), calls=%async_computation.4 | async-start | bytes 4718592 | tf_op jit(solution)/shard_map/all_gather | solution.py:139
  126.5 10.7 copy-start.32
  129.6 9.7 copy-start.1
  139.3 18.5 %copy-start.5 = (bf16[256,1024]{1,0:T(8,128)(2,1)S(1)}, bf16[256,1024]{1,0:T(8,128)(2,1)}, u32[]{:S(2)}) copy-start(bf16[256,1024]{1,0:T(8,128)(2,1)} %param.22) | copy-start | bytes 1572868
  139.3 277.6 %all-gather.17.cloned.1.call-start = ((), (), s32[]{:S(2)}) async-start(), calls=%async_computation.7 | async-start | bytes 9437184 | tf_op jit(solution)/shard_map/all_gather | solution.py:94
  140.4 379.5 %all-gather.19.cloned.1.call-start = ((), (), s32[]{:S(2)}) async-start(), calls=%async_computation.8 | async-start | bytes 9437184 | tf_op jit(solution)/shard_map/all_gather | solution.py:95
  143.2 568.8 %reduce-scatter.6.cloned.1.call-start = ((), (), s32[]{:S(2)}) async-start(), calls=%async_computation.9 | async-start | bytes 18874368 | tf_op jit(solution)/shard_map/reduce_scatter | solution.py:213
  416.8 824.6 %reduce-scatter.8.cloned.1.call-start = ((), (), s32[]{:S(2)}) async-start(), calls=%async_computation.10 | async-start | bytes 56623104 | tf_op jit(solution)/shard_map/reduce_scatter | solution.py:241
  520.0 15.2 %copy-start.17 = (f32[256,4096]{1,0:T(8,128)S(1)}, f32[256,4096]{1,0:T(8,128)}, u32[]{:S(2)}) copy-start(f32[256,4096]{1,0:T(8,128)} %convolution_add_fusion) | copy-start | bytes 12582916
  535.2 8.9 copy-start.27
  573.4 143.7 %copy-start.29 = (f32[1,1024]{1,0:T(1,128)S(1)}, f32[1,1024]{1,0:T(1,128)}, u32[]{:S(2)}) copy-start(f32[1,1024]{1,0:T(1,128)} %copy-done.28) | copy-start | bytes 12292
  573.4 143.7 %copy-start.31 = (f32[1,1024]{1,0:T(1,128)S(1)}, f32[1,1024]{1,0:T(1,128)}, u32[]{:S(2)}) copy-start(f32[1,1024]{1,0:T(1,128)} %copy-done.30) | copy-start | bytes 12292
  712.0 5.1 copy-start.35
  757.2 558.1 %reduce-scatter.10.cloned.1.call-start = ((), (), s32[]{:S(2)}) async-start(), calls=%async_computation.12 | async-start | bytes 589824
  757.2 6.5 copy-start.9
  757.3 6.5 copy-start.12
  757.3 6.5 copy-start.15
  763.8 5.4 copy-start.18
  763.8 5.3 copy-start.42
  763.8 5.3 copy-start.36
  770.2 471.3 %copy-start.49 = (u32[128]{0:T(128)S(1)}, u32[128]{0:T(128)}, u32[]{:S(2)}) copy-start(u32[128]{0:T(128)} %constant.34) | copy-start | bytes 1540
  771.2 700.8 %all-reduce.4.cloned.1.call-start = ((), (), s32[]{:S(2)}) async-start(), calls=%async_computation.11 | async-start | bytes 12582912 | tf_op jit(solution)/shard_map/psum | solution.py:259
  1243.4 6.0 copy-start.4
  1243.4 6.0 copy-start.22
  1251.0 118.6 %copy-start.46 = (f32[4,128]{1,0:T(4,128)S(1)}, f32[4,128]{1,0:T(4,128)}, u32[]{:S(2)}) copy-start(f32[4,128]{1,0:T(4,128)} %param.28) | copy-start | bytes 6148
  1251.0 118.6 %copy-start.47 = (f32[4,128]{1,0:T(4,128)S(1)}, f32[4,128]{1,0:T(4,128)}, u32[]{:S(2)}) copy-start(f32[4,128]{1,0:T(4,128)} %param.38) | copy-start | bytes 6148
  1251.0 118.6 %copy-start.48 = (f32[4,128]{1,0:T(4,128)S(1)}, f32[4,128]{1,0:T(4,128)}, u32[]{:S(2)}) copy-start(f32[4,128]{1,0:T(4,128)} %param.39) | copy-start | bytes 6148
  1251.0 119.2 %copy-start.38 = (f32[1152]{0:T(1024)S(1)}, f32[1152]{0:T(1024)}, u32[]{:S(2)}) copy-start(f32[1152]{0:T(1024)} %param.29) | copy-start | bytes 13828
  1251.0 119.2 %copy-start.43 = (f32[1152]{0:T(1024)S(1)}, f32[1152]{0:T(1024)}, u32[]{:S(2)}) copy-start(f32[1152]{0:T(1024)} %param.40) | copy-start | bytes 13828
  1251.0 119.2 %copy-start.44 = (f32[1152]{0:T(1024)S(1)}, f32[1152]{0:T(1024)}, u32[]{:S(2)}) copy-start(f32[1152]{0:T(1024)} %param.41) | copy-start | bytes 13828
  1251.0 221.0 %copy-start.7 = (f32[128,3072]{1,0:T(8,128)S(1)}, f32[128,3072]{1,0:T(8,128)}, u32[]{:S(2)}) copy-start(f32[128,3072]{1,0:T(8,128)} %param.24) | copy-start | bytes 4718596
  1251.6 226.1 %copy-start.26 = (f32[128,1024]{1,0:T(8,128)S(1)}, f32[128,1024]{1,0:T(8,128)}, u32[]{:S(2)}) copy-start(f32[128,1024]{1,0:T(8,128)} %param.25) | copy-start | bytes 1572868
  1472.0 5.6 copy-start.6
  1472.0 9.0 copy-start.3
  1472.0 9.0 copy-start.24
  1472.0 9.0 copy-start.25
  (12 other events, 23.5 us)
Sparse Core Ops, SparseCore 0:
  10.9 92.0 all-gather.8
  105.9 51.7 all-gather.14
  160.7 69.3 all-gather.12
  232.6 71.5 all-gather.10
  307.0 105.0 all-gather.16
  414.9 105.0 all-gather.18
  523.9 188.0 reduce-scatter.5
  757.3 484.0 reduce-scatter.7
  1245.5 69.7 reduce-scatter.9
  1317.8 154.1 all-reduce.3
where the time goes:
time: 1500 us
  waiting for transfers between devices  1030 us (69%)
  matrix products  176 us (12%)
  blocking collectives  152 us (10%)
  other arithmetic  97.9 us (7%)
  local copies, waits for them, and re-layouts  28.2 us (2%)
  between operations  15.9 us (1%)
    reduce_scatter x1, waiting for transfers between devices, body(): lax.psum_scatter(jnp.concatenate([contract_rows(normed_one, grad_qkv), co...  470 us
    reduce_scatter x1, waiting for transfers between devices, body(): lax.psum_scatter(key_terms, 'shard', scatter_dimension=0, tiled=True)  139 us
    psum x1, waiting for transfers between devices, body(): lax.psum((matrix_grad, norm_part, bias_part), 'rep')  101 us
    all_gather x1, waiting for transfers between devices, body(): lax.all_gather(w_down.astype(jnp.bfloat16), 'shard', axis=0, tiled=True)  95.3 us
    all_gather x1, waiting for transfers between devices, body(): lax.all_gather(value_flat, 'shard', axis=0, tiled=True)  68.8 us
    all_gather x1, waiting for transfers between devices, body(): lax.all_gather(key_flat, 'shard', axis=0, tiled=True)  67.8 us
    psum x1, blocking collectives, body(): lax.psum((matrix_grad, norm_part, bias_part), 'rep')  53.4 us
    all_gather x1, waiting for transfers between devices, body(): lax.all_gather(w_qkv.astype(jnp.bfloat16), 'shard', axis=0, tiled=True)  41 us
  transfers between devices with their start and end apart: 10, of which 9 were waited for; matrix products, arithmetic and copies ran while one was open for 16% of the time, Pallas kernels for 0%

commit v1 on v0

v1 whole, which is shorter than its diff:
```python
import functools

import jax
import jax.numpy as jnp
import numpy as np
from jax import lax
from jax.experimental import pallas as pl
from jax.experimental.pallas import tpu as pltpu
from jax.sharding import PartitionSpec as P

HEAD_DIM = 64
ROT = 16
STEP = 10
EPS_NORM = 1e-05
BETA_ONE = 0.9
BETA_TWO = 0.95
RATE_MATRIX = 0.05
RATE_VECTOR = 0.3
DECAY = 0.01
ADAM_EPS = 1e-08
NEGATIVE = -1e30

NY, NXL, NC, NXH, NZ = 4, 2, 2, 2, 4
AXES = ("rep", "shard")
D = 1024
ROWS = 256
SEQ = 2048
FF = 4096
PAIR = 128
HID = 512
QB = 512
BF = jnp.bfloat16
F32 = jnp.float32


def device_pairs(move):
    pairs = []
    for y in range(NY):
        for xl in range(NXL):
            for c in range(NC):
                for h in range(NXH):
                    for z in range(NZ):
                        ty, txl, tc, th, tz = move(y, xl, c, h, z)
                        pairs.append(
                            (
                                ((y * NXL + xl) * NC + c) * 8 + h * NZ + z,
                                ((ty * NXL + txl) * NC + tc) * 8 + th * NZ + tz % NZ,
                            )
                        )
    return pairs


def spread_pairs(k):
    def move(y, xl, c, h, z):
        return (y, xl, h, c, z + k)

    return device_pairs(move)


SPREAD = [spread_pairs(k) for k in range(NZ)]
COLLECT = [[(t, s) for s, t in pairs] for pairs in SPREAD]
SIBLING = device_pairs(lambda y, xl, c, h, z: (y, xl, 1 - c, h, z))
ROUND_Z = [device_pairs(lambda y, xl, c, h, z, k=k: (y, xl, c, h, z + k)) for k in range(NZ)]


def device(y, xl, c, h, z):
    return ((y * NXL + xl) * NC + c) * 8 + h * NZ + z


RANGES = dict(y=range(NY), xl=range(NXL), c=range(NC), h=range(NXH), z=range(NZ))


def groups(*inner):
    outer = [name for name in RANGES if name not in inner]

    def walk(names, at):
        if not names:
            return [device(**at)]
        return [d for n in RANGES[names[0]] for d in walk(names[1:], dict(at, **{names[0]: n}))]

    def each(names, at):
        if not names:
            return [walk(inner, at)]
        return [g for n in RANGES[names[0]] for g in each(names[1:], dict(at, **{names[0]: n}))]

    return each(outer, {})


ALONG_Y = groups("y")
ALONG_Z = groups("z")
PLANE = groups("h", "y", "xl")
COPIES = groups("y", "xl")
SAME_CORE = groups("h", "z", "y", "xl")


def spread(blocks):
    return [lax.ppermute(b, AXES, SPREAD[k]) for k, b in enumerate(blocks)]


def collect(blocks):
    return [lax.ppermute(b, AXES, COLLECT[k]) for k, b in enumerate(blocks)]


def sibling(values):
    return lax.ppermute(values, AXES, SIBLING)


def exchange(values, members):
    return lax.all_to_all(values, AXES, 0, 0, axis_index_groups=members, tiled=True)


def dot(a, b, ca, cb):
    return lax.dot_general(a, b, (((ca,), (cb,)), ((), ())), preferred_element_type=F32)


def gelu_parts(values):
    cdf = 0.5 * (1.0 + lax.erf(values * np.float32(np.sqrt(0.5))))
    density = jnp.exp(-0.5 * values * values) * np.float32(1.0 / np.sqrt(2.0 * np.pi))
    return values * cdf, cdf + values * density


def adam_step(weight, moment, square, gradient, rate, decay):
    moment_new = BETA_ONE * moment + (1.0 - BETA_ONE) * gradient
    square_new = BETA_TWO * square + (1.0 - BETA_TWO) * gradient * gradient
    fixed_moment = moment_new / (1.0 - BETA_ONE**STEP)
    fixed_square = square_new / (1.0 - BETA_TWO**STEP)
    weight_new = weight - rate * (
        fixed_moment / (jnp.sqrt(fixed_square) + ADAM_EPS) + decay * weight
    )
    return (weight_new, moment_new, square_new)


SM = pl.BlockSpec(memory_space=pltpu.SMEM)
VM = pl.BlockSpec(memory_space=pltpu.VMEM)


def params(mib=16):
    return pltpu.CompilerParams(vmem_limit_bytes=mib * 2**20)


def cost(us):
    flops = int(us * 7e8)
    return pl.CostEstimate(flops=flops, bytes_accessed=int(us * 2e6), transcendentals=0)


def shape(dims, kind):
    return jax.ShapeDtypeStruct(dims, kind)


def send_weights_kernel(
    where_ref, w_ref, up_ref, down_ref, norm_ref, bias_ref, seg_ref, sib_ref, out_ref
):
    core = where_ref[0]
    misc = jnp.concatenate(
        [norm_ref[...], bias_ref[...], seg_ref[...].astype(F32), jnp.zeros((1, 128), F32)], axis=0
    ).astype(BF)
    theirs = jnp.concatenate([sib_ref[...].astype(F32), jnp.zeros((14, 128), F32)], axis=0).astype(BF)
    rows = pl.ds(pl.multiple_of(where_ref[2] * 32, 32), 32)
    for n in range(8):
        for part in range(3):
            source = pl.multiple_of(part * D + core * 512 + (n % NZ) * PAIR, PAIR)
            lanes = slice(part * PAIR, (part + 1) * PAIR)
            out_ref[n, 0:128, lanes] = w_ref[:, pl.ds(source, PAIR)].astype(BF)
        out_ref[n, 128:144, 0:128] = misc
        out_ref[n, 128:144, 128:256] = theirs
        out_ref[n, 128:144, 256:384] = jnp.zeros((16, 128), BF)
        for j in range(8):
            ref = (up_ref, down_ref)[j // 4]
            source = pl.multiple_of(core * 2048 + (n % NZ) * HID + (j % 4) * 128, 128)
            first = 144 + (j // 3) * 32
            out_ref[n, first : first + 32, (j % 3) * 128 : (j % 3 + 1) * 128] = ref[
                rows, pl.ds(source, 128)
            ].astype(BF)
        out_ref[n, 208:240, 256:384] = jnp.zeros((32, 128), BF)


def send_weights(where, w, up, down, norms, biases, segments, sibling_segments):
    return pl.pallas_call(
        send_weights_kernel,
        in_specs=[SM] + [VM] * 7,
        out_specs=VM,
        out_shape=shape((8, 240, 384), BF),
        compiler_params=params(),
        cost_estimate=cost(0),
        name="send_weights",
    )(where, w, up, down, norms, biases, segments, sibling_segments)


def join_kernel(*refs):
    for k in range(NZ):
        refs[NZ][k * ROWS : (k + 1) * ROWS, :] = refs[k][0:ROWS, :]


def join(blocks, us):
    return pl.pallas_call(
        join_kernel,
        in_specs=[VM] * NZ,
        out_specs=VM,
        out_shape=shape((SEQ // 2, D), BF),
        compiler_params=params(),
        cost_estimate=cost(us),
        name="join",
    )(*blocks)


def doc_start(ids, meta_ref):
    start = jnp.zeros_like(ids)
    for d in range(4):
        start = jnp.where(ids >= meta_ref[d], meta_ref[d], start)
    return start


def block_tables(where_ref, meta_ref):
    c, z = where_ref[0], where_ref[1]
    meta_ref[4] = c
    meta_ref[5] = z
    meta_ref[6] = c * NZ + z
    meta_ref[7] = where_ref[2]
    for j in range(2):
        half = c if j == 0 else 1 - c
        for k in range(NZ):
            meta_ref[8 + j * NZ + k] = half * NZ + jnp.bitwise_and(z + NZ - k, NZ - 1)
    for half in range(2):
        base = jnp.bitwise_xor(c, half) * NZ
        for ring in range(NZ):
            meta_ref[16 + half * NZ + ring] = base + jnp.bitwise_and(z + NZ - ring, NZ - 1)


def assemble_kernel(
    where_ref, in_ref, w_ref, norm_ref, bias_ref, ffn_ref, meta_ref
):
    block_tables(where_ref, meta_ref)
    counts = [jnp.zeros((1, 128), F32) for _ in range(4)]
    native = (where_ref[0] == where_ref[3]).astype(F32)
    for n in range(8):
        w_ref[n * 128 : (n + 1) * 128, :] = in_ref[n, 0:128, :]
        misc = in_ref[n, 128:144, 0:128].astype(F32)
        other = in_ref[n, 128:144, 128:256].astype(F32)
        norm_ref[:, n * 128 : (n + 1) * 128] = misc[0:4]
        bias_ref[n * 9 : (n + 1) * 9, :] = misc[4:13]
        docs = misc[13:15] * native + other[0:2] * (1.0 - native)
        for d in range(4):
            below = jnp.where(docs < d + 0.5, 1.0, 0.0)
            counts[d] = counts[d] + below[0:1] + below[1:2]
        for j in range(8):
            first = 144 + (j // 3) * 32
            block = in_ref[n, first : first + 32, (j % 3) * 128 : (j % 3 + 1) * 128]
            for y in range(NY):
                ffn_ref[y, n * 32 : (n + 1) * 32, j * 128 : (j + 1) * 128] = block
    for d in range(4):
        meta_ref[d] = jnp.sum(counts[d]).astype(jnp.int32)


def rotary_tables():
    lane = np.arange(PAIR) % HEAD_DIM
    freq = 10000.0 ** (-2.0 * (lane % (ROT // 2)) / ROT)
    angles = np.arange(SEQ)[:, None] * np.where(lane < ROT, freq, 0.0)[None, :]
    return jnp.asarray(np.cos(angles), F32), jnp.asarray(np.sin(angles), F32)


def assemble(where, received):
    return pl.pallas_call(
        assemble_kernel,
        in_specs=[SM, VM],
        out_specs=[VM] * 4 + [SM],
        out_shape=[
            shape((D, 3 * PAIR), BF),
            shape((4, D), F32),
            shape((72, 128), F32),
            shape((NY, ROWS, 2 * HID), BF),
            shape((24,), jnp.int32),
        ],
        compiler_params=params(),
        cost_estimate=cost(0),
        name="assemble",
    )(where, received)


def assemble_ffn_kernel(in_ref, up_ref, down_ref):
    for y in range(NY):
        for n in range(8):
            rows = slice(n * 128 + y * 32, n * 128 + (y + 1) * 32)
            up_ref[rows, :] = in_ref[y, n * 32 : (n + 1) * 32, 0:HID]
            down_ref[rows, :] = in_ref[y, n * 32 : (n + 1) * 32, HID:]


def assemble_ffn(parts):
    return pl.pallas_call(
        assemble_ffn_kernel,
        in_specs=[VM],
        out_specs=[VM] * 2,
        out_shape=[shape((D, HID), BF)] * 2,
        compiler_params=params(),
        cost_estimate=cost(0),
        name="assemble_ffn",
    )(parts)


def turn(u, cosine, sine):
    lane = lax.broadcasted_iota(jnp.int32, u.shape, 1) % HEAD_DIM
    left = pltpu.roll(u, PAIR - ROT // 2, 1)
    right = pltpu.roll(u, ROT // 2, 1)
    return u * cosine + jnp.where(lane < ROT // 2, -left, right) * sine


def qkv_kernel(meta_ref, x_ref, w_ref, bias_ref, norm_ref, cos_ref, sin_ref, *refs):
    n2_ref, xh_ref, q_ref, k_ref, v_ref = refs[-5:]
    x = x_ref[...].astype(F32)
    centred = x - jnp.mean(x, axis=-1, keepdims=True)
    variance = jnp.mean(centred * centred, axis=-1, keepdims=True)
    xh = centred * lax.rsqrt(variance + EPS_NORM)
    n1 = (xh * norm_ref[0:1, :] + norm_ref[1:2, :]).astype(BF)
    xh_ref[...] = xh.astype(BF)
    n2_ref[...] = (xh * norm_ref[2:3, :] + norm_ref[3:4, :]).astype(BF)
    part = meta_ref[6]
    cosine, sine = cos_ref[...], sin_ref[...]
    qkv = dot(n1, w_ref[...], 1, 0)
    q = qkv[:, 0:PAIR] + bias_ref[pl.ds(part, 1), :]
    k = qkv[:, PAIR : 2 * PAIR] + bias_ref[pl.ds(8 + part, 1), :]
    v = qkv[:, 2 * PAIR :] + bias_ref[pl.ds(16 + part, 1), :]
    q_ref[...] = (turn(q, cosine, sine).astype(BF) * 0.125).astype(BF)
    k_ref[...] = turn(k, cosine, sine).astype(BF)
    v_ref[...] = v.astype(BF)


def project_qkv(meta, x, w, bias, norms, cosine, sine, before, us):
    base = 0 if before is None else NZ
    moving = lambda i, meta: (i, 0)
    physical = lambda i, meta: (base + i, 0)
    logical = lambda i, meta: (meta[8 + base + i], 0)
    fixed = lambda i, meta: (0, 0)
    extra = [] if before is None else list(before)
    return pl.pallas_call(
        qkv_kernel,
        grid_spec=pltpu.PrefetchScalarGridSpec(
            num_scalar_prefetch=1,
            grid=(NZ,),
            in_specs=[
                pl.BlockSpec((ROWS, D), moving),
                pl.BlockSpec((D, 3 * PAIR), fixed),
                pl.BlockSpec((72, 128), fixed),
                pl.BlockSpec((4, D), fixed),
                pl.BlockSpec((ROWS, PAIR), logical),
                pl.BlockSpec((ROWS, PAIR), logical),
            ]
            + [pl.BlockSpec(memory_space=pl.ANY)] * len(extra),
            out_specs=[pl.BlockSpec((ROWS, D), physical)] * 2
            + [pl.BlockSpec((ROWS, PAIR), logical)] * 3,
        ),
        out_shape=[shape((SEQ, D), BF)] * 2 + [shape((SEQ, PAIR), BF)] * 3,
        input_output_aliases={7 + n: n for n in range(len(extra))},
        compiler_params=params(),
        cost_estimate=cost(us),
        name="project_qkv",
    )(meta, x, w, bias, norms, cosine, sine, *extra)


def head_only(values, h):
    lane = lax.broadcasted_iota(jnp.int32, values.shape, 1)
    return jnp.where((lane // HEAD_DIM) == h, values, jnp.zeros_like(values))


def tile_mask(meta_ref, i, j):
    keys = j * QB + lax.broadcasted_iota(jnp.int32, (QB, QB), 0)
    query_row = i * QB + lax.broadcasted_iota(jnp.int32, (1, QB), 1)
    start = doc_start(query_row, meta_ref)
    return (keys <= query_row) & (keys >= start)


def attn_forward_kernel(meta_ref, q_ref, k_ref, v_ref, ctx_ref, ctxt_ref, stat_ref, vt_ref):
    i = pl.program_id(0)

    @pl.when(i == 0)
    def _():
        for b in range(SEQ // QB):
            vt_ref[:, b * QB : (b + 1) * QB] = v_ref[b * QB : (b + 1) * QB, :].T

    q = q_ref[pl.ds(pl.multiple_of(i * QB, QB), QB), :]
    heads = [head_only(q, h) for h in range(2)]

    def step(j, carry):
        mask = tile_mask(meta_ref, i, j)
        row = pl.multiple_of(j * QB, QB)
        keys = k_ref[pl.ds(row, QB), :]
        out = []
        for h in range(2):
            m, l, acc = carry[h]
            scores = dot(keys, heads[h], 1, 1)
            scores = jnp.where(mask, scores, NEGATIVE)
            top = jnp.maximum(m, jnp.max(scores, axis=0, keepdims=True))
            expo = jnp.exp(scores - top)
            fade = jnp.exp(m - top)
            l = l * fade + jnp.sum(expo, axis=0, keepdims=True)
            values = vt_ref[h * HEAD_DIM : (h + 1) * HEAD_DIM, pl.ds(row, QB)]
            acc = acc * fade + dot(values, expo.astype(BF), 1, 0)
            out.append((top, l, acc))
        return tuple(out)

    zero = (
        jnp.full((1, QB), NEGATIVE, F32),
        jnp.zeros((1, QB), F32),
        jnp.zeros((HEAD_DIM, QB), F32),
    )
    result = lax.fori_loop(0, i + 1, step, (zero, zero))
    column = pl.multiple_of(i * QB, QB)
    parts = []
    for h in range(2):
        m, l, acc = result[h]
        parts.append(acc / l)
        stat_ref[h : h + 1, pl.ds(column, QB)] = m
        stat_ref[2 + h : 3 + h, pl.ds(column, QB)] = 1.0 / l
    ctxt = jnp.concatenate(parts, axis=0)
    ctxt_ref[:, pl.ds(column, QB)] = ctxt
    low = ctxt.astype(BF).T
    for b in range(QB // ROWS):
        row = pl.multiple_of(meta_ref[16 + i * (QB // ROWS) + b] * ROWS, ROWS)
        ctx_ref[pl.ds(row, ROWS), :] = low[b * ROWS : (b + 1) * ROWS]


def attn_forward(meta, q, k, v):
    return pl.pallas_call(
        attn_forward_kernel,
        grid=(SEQ // QB,),
        in_specs=[SM, VM, VM, VM],
        out_specs=[VM, VM, VM],
        out_shape=[shape((SEQ, PAIR), BF), shape((PAIR, SEQ), F32), shape((8, SEQ), F32)],
        scratch_shapes=[pltpu.VMEM((PAIR, SEQ), BF)],
        compiler_params=params(),
        cost_estimate=cost(0),
        name="attn_forward",
    )(meta, q, k, v)


def attn_prepare_kernel(
    q_ref, k_ref, dctx_ref, ctxt_ref, stat_ref, kt_ref, du_ref, dut_ref, qh_ref, c_ref
):
    c_ref[...] = jnp.zeros_like(c_ref)
    for b in range(SEQ // QB):
        cols = slice(b * QB, (b + 1) * QB)
        kt_ref[:, cols] = k_ref[cols, :].T
        dctxt = dctx_ref[cols, :].T
        prod = dctxt * ctxt_ref[:, cols]
        for h in range(2):
            rows = slice(h * HEAD_DIM, (h + 1) * HEAD_DIM)
            inverse = stat_ref[2 + h : 3 + h, cols]
            c_ref[h : h + 1, cols] = jnp.sum(prod[rows], axis=0, keepdims=True) * inverse
            dut = (dctxt[rows] * inverse).astype(BF)
            dut_ref[h, rows, cols] = dut
            dut_ref[h, (1 - h) * HEAD_DIM : (2 - h) * HEAD_DIM, cols] = jnp.zeros_like(dut)
        for h in range(2):
            du_ref[h, cols, :] = dut_ref[h, :, cols].T
            qh_ref[h, cols, :] = head_only(q_ref[cols, :], h)


def attn_prepare(q, k, dctx, ctxt, stat):
    return pl.pallas_call(
        attn_prepare_kernel,
        in_specs=[VM] * 5,
        out_specs=[VM] * 5,
        out_shape=[
            shape((PAIR, SEQ), BF),
            shape((2, SEQ, PAIR), BF),
            shape((2, PAIR, SEQ), BF),
            shape((2, SEQ, PAIR), BF),
            shape((8, SEQ), F32),
        ],
        compiler_params=params(),
        cost_estimate=cost(60),
        name="attn_prepare",
    )(q, k, dctx, ctxt, stat)


def attn_backward_kernel(
    meta_ref, k_ref, v_ref, stat_ref, cos_ref, sin_ref, kt_ref, du_ref, dut_ref, qh_ref, c_ref,
    out_ref,
    dqt_ref, dk_ref, dv_ref,
):
    j = pl.program_id(0)
    blocks = SEQ // QB

    @pl.when(j == 0)
    def _():
        dqt_ref[...] = jnp.zeros_like(dqt_ref)

    row = pl.multiple_of(j * QB, QB)
    keys = k_ref[pl.ds(row, QB), :]
    values = v_ref[pl.ds(row, QB), :]

    def step(i, carry):
        dk, dv = carry
        mask = tile_mask(meta_ref, i, j)
        col = pl.multiple_of(i * QB, QB)
        for h in range(2):
            qh = qh_ref[h, pl.ds(col, QB), :]
            scores = dot(keys, qh, 1, 1)
            m = stat_ref[h : h + 1, pl.ds(col, QB)]
            expo = jnp.where(mask, jnp.exp(scores - m), 0.0)
            dexpo = dot(values, dut_ref[h, :, pl.ds(col, QB)], 1, 0)
            dscore = (expo * (dexpo - c_ref[h : h + 1, pl.ds(col, QB)])).astype(BF)
            dv = dv + dot(expo.astype(BF), du_ref[h, pl.ds(col, QB), :], 1, 0)
            dk = dk + dot(dscore, qh, 1, 0)
            rows = slice(h * HEAD_DIM, (h + 1) * HEAD_DIM)
            dqt_ref[rows, pl.ds(col, QB)] += dot(kt_ref[rows, pl.ds(row, QB)], dscore, 1, 0)
        return dk, dv

    zero = jnp.zeros((QB, PAIR), F32)
    dk, dv = lax.fori_loop(j, blocks, step, (zero, zero))
    dk_ref[pl.ds(row, QB), :] = dk
    dv_ref[pl.ds(row, QB), :] = dv

    @pl.when(j == blocks - 1)
    def _():
        for b in range(SEQ // ROWS):
            rows = slice(b * ROWS, (b + 1) * ROWS)
            place = pl.ds(pl.multiple_of(meta_ref[16 + b] * ROWS, ROWS), ROWS)
            cosine, sine = cos_ref[rows, :], -sin_ref[rows, :]
            dq = (dqt_ref[:, rows] * 0.125).T
            out_ref[place, 0:PAIR] = turn(dq, cosine, sine).astype(BF)
            out_ref[place, PAIR : 2 * PAIR] = turn(dk_ref[rows, :], cosine, sine).astype(BF)
            out_ref[place, 2 * PAIR :] = dv_ref[rows, :].astype(BF)


def attn_backward(meta, k, v, stat, cosine, sine, prepared):
    return pl.pallas_call(
        attn_backward_kernel,
        grid=(SEQ // QB,),
        in_specs=[SM] + [VM] * 10,
        out_specs=VM,
        out_shape=shape((SEQ, 3 * PAIR), BF),
        scratch_shapes=[
            pltpu.VMEM((PAIR, SEQ), F32),
            pltpu.VMEM((SEQ, PAIR), F32),
            pltpu.VMEM((SEQ, PAIR), F32),
        ],
        compiler_params=params(),
        cost_estimate=cost(100),
        name="attn_backward",
    )(meta, k, v, stat, cosine, sine, *prepared)


def lay_rows(ref, first, count):
    return jnp.concatenate([ref[pl.ds(first + r, 1), :] for r in range(count)], axis=1)


def by_half(double):
    return [
        pl.BlockSpec((double, D), lambda i, meta: (jnp.minimum(i, 1), 0)),
        pl.BlockSpec((double, D), lambda i, meta: (jnp.maximum(i - 2, 0), 0)),
    ]


def take_half(step, mine_ref, theirs_ref, now_ref):
    @pl.when(step < 2)
    def _():
        now_ref[...] = mine_ref[...]

    @pl.when(step >= 2)
    def _():
        now_ref[...] = theirs_ref[...]


def ffn_kernel(meta_ref, *refs):
    mine_ref, theirs_ref = refs[:2]
    n2_ref, xh_ref, ctx_ref, up_ref, down_ref, proj_ref, bias_ref, norm_ref = refs[2:10]
    out_mine_ref, out_theirs_ref, back_ref, dctx_ref, vec_ref, grad_ref = refs[10:16]
    dy_now, gup, gdown, gproj, total = refs[16:]
    step = pl.program_id(0)
    part = meta_ref[6]

    @pl.when(step == 0)
    def _():
        gup[...] = jnp.zeros_like(gup)
        gdown[...] = jnp.zeros_like(gdown)
        gproj[...] = jnp.zeros_like(gproj)
        total[...] = jnp.zeros_like(total)

    take_half(step, mine_ref, theirs_ref, dy_now)
    dy = dy_now[...]
    ctx = ctx_ref[...]
    dctx = dot(dy, proj_ref[...], 1, 1)
    for b in range(2):
        row = pl.multiple_of(meta_ref[8 + 2 * step + b] * ROWS, ROWS)
        dctx_ref[pl.ds(row, ROWS), :] = dctx[b * ROWS : (b + 1) * ROWS]
    gproj[...] += dot(ctx, dy, 0, 0)
    bias_up = lay_rows(bias_ref, 32 + 4 * part, 4)
    pre = dot(n2_ref[...], up_ref[...], 1, 0) + bias_up
    hidden, slope = gelu_parts(pre)
    hidden = hidden.astype(BF)
    dpre = (dot(dy, down_ref[...], 1, 0) * slope).astype(BF)
    out = (dot(ctx, proj_ref[...], 1, 0) + dot(hidden, down_ref[...], 1, 1)).astype(BF)

    @pl.when(step < 2)
    def _():
        out_mine_ref[...] = out

    @pl.when(step >= 2)
    def _():
        out_theirs_ref[...] = out

    back_ref[...] = (dot(dpre, up_ref[...], 1, 1) * norm_ref[2:3, :]).astype(BF)
    gdown[...] += dot(dy, hidden, 0, 0)
    gup[...] += dot(xh_ref[...], dpre, 0, 0)
    total[...] += jnp.broadcast_to(jnp.sum(dpre.astype(F32), axis=0, keepdims=True), total.shape)

    @pl.when(step == 3)
    def _():
        sums = total[...]
        raw = gup[...]
        gain = jnp.transpose(jnp.broadcast_to(norm_ref[2:3, :], (8, D)))[:, 0:1]
        shift = jnp.transpose(jnp.broadcast_to(norm_ref[3:4, :], (8, D)))[:, 0:1]
        product = (raw * up_ref[...].astype(F32)).astype(BF)
        gup[...] = raw * gain + shift * sums[0:1, :]
        for h in range(NXH):
            for p in range(8):
                for ring in range(NZ):
                    first = h * 512 + ring * 128 + p * 16
                    here = slice(ring * 16, (ring + 1) * 16)
                    grad_ref[h * 8 + p, here, 0:HID] = gup[first : first + 16, :].astype(BF)
                    grad_ref[h * 8 + p, here, HID:] = gdown[first : first + 16, :].astype(BF)
                grad_ref[h * 8 + p, 64:80, :] = gproj[p * 16 : (p + 1) * 16, :].astype(BF)
        vec_ref[0:8, :] = dot(jnp.ones((8, HID), BF), product, 1, 1)
        vec_ref[8:16, :] = dot(sums.astype(BF), up_ref[...], 1, 1)
        vec_ref[16:24, 0:HID] = sums
        vec_ref[16:24, HID:] = jnp.zeros((8, D - HID), F32)


def feed_forward(meta, mine, theirs, n2, xh, ctx, up, down, proj, bias, norms):
    double = 2 * ROWS
    moving = lambda i, meta: (i, 0)
    fixed = lambda i, meta: (0, 0)
    once = pl.Buffered(1)
    return pl.pallas_call(
        ffn_kernel,
        grid_spec=pltpu.PrefetchScalarGridSpec(
            num_scalar_prefetch=1,
            grid=(4,),
            in_specs=by_half(double)
            + [
                pl.BlockSpec((double, D), moving),
                pl.BlockSpec((double, D), moving),
                pl.BlockSpec((double, PAIR), moving),
                pl.BlockSpec((D, HID), fixed, pipeline_mode=once),
                pl.BlockSpec((D, HID), fixed, pipeline_mode=once),
                pl.BlockSpec((PAIR, D), lambda i, meta: (2, 0), pipeline_mode=once),
                pl.BlockSpec((72, 128), fixed, pipeline_mode=once),
                pl.BlockSpec((4, D), fixed, pipeline_mode=once),
            ],
            out_specs=by_half(double)
            + [
                pl.BlockSpec((double, D), moving),
                VM,
                VM,
                VM,
            ],
            scratch_shapes=[
                pltpu.VMEM((double, D), BF),
                pltpu.VMEM((D, HID), F32),
                pltpu.VMEM((D, HID), F32),
                pltpu.VMEM((PAIR, D), F32),
                pltpu.VMEM((8, HID), F32),
            ],
        ),
        out_shape=[
            shape((SEQ // 2, D), BF),
            shape((SEQ // 2, D), BF),
            shape((SEQ, D), BF),
            shape((SEQ, PAIR), F32),
            shape((24, D), F32),
            shape((16, 80, 2 * HID), BF),
        ],
        compiler_params=params(32),
        cost_estimate=cost(60),
        name="feed_forward",
    )(meta, mine, theirs, n2, xh, ctx, up, down, proj, bias, norms)


def core_sum_kernel(mine_ref, theirs_ref, *sent_refs):
    step = pl.program_id(0)
    total = (mine_ref[...].astype(F32) + theirs_ref[...].astype(F32)).astype(BF)
    for k in range(NZ):

        @pl.when(step == k)
        def _():
            sent_refs[k][...] = total


def core_sum(mine, theirs):
    moving = lambda i: (i, 0)
    return pl.pallas_call(
        core_sum_kernel,
        grid=(NZ,),
        in_specs=[pl.BlockSpec((ROWS, D), moving)] * 2,
        out_specs=[pl.BlockSpec((ROWS, D), lambda i: (0, 0))] * NZ,
        out_shape=[shape((ROWS, D), BF)] * NZ,
        compiler_params=params(),
        cost_estimate=cost(0),
        name="core_sum",
    )(mine, theirs)


def finish_out_kernel(x_ref, bias_ref, *refs):
    bias = lay_rows(bias_ref, 24, 8) + lay_rows(bias_ref, 64, 8)
    total = refs[0][...].astype(F32)
    for k in range(1, NZ):
        total = total + refs[k][...].astype(F32)
    refs[NZ][...] = (x_ref[...].astype(F32) + total + bias).astype(BF)


def finish_out(x, bias, pieces):
    return pl.pallas_call(
        finish_out_kernel,
        in_specs=[VM] * (2 + NZ),
        out_specs=VM,
        out_shape=shape((ROWS, D), BF),
        compiler_params=params(),
        cost_estimate=cost(0),
        name="finish_out",
    )(x, bias, *pieces)


def finish_grad_kernel(x_ref, dy_ref, *refs):
    w = refs[0][...].astype(F32)
    for k in range(1, NZ):
        w = w + refs[k][...].astype(F32)
    x = x_ref[...].astype(F32)
    centred = x - jnp.mean(x, axis=-1, keepdims=True)
    rstd = lax.rsqrt(jnp.mean(centred * centred, axis=-1, keepdims=True) + EPS_NORM)
    xh = centred * rstd
    inner = w - jnp.mean(w, axis=-1, keepdims=True) - xh * jnp.mean(w * xh, axis=-1, keepdims=True)
    refs[NZ][...] = dy_ref[...].astype(F32) + rstd * inner


def finish_grad(x, dy, pieces):
    return pl.pallas_call(
        finish_grad_kernel,
        in_specs=[VM] * (2 + NZ),
        out_specs=VM,
        out_shape=shape((ROWS, D), F32),
        compiler_params=params(),
        cost_estimate=cost(0),
        name="finish_grad",
    )(x, dy, *pieces)


def ffn_reduce_kernel(where_ref, in_ref, own_ref, *sent_refs):
    z = where_ref[1]
    total = in_ref[0].astype(F32)
    for n in range(1, 16):
        total = total + in_ref[n].astype(F32)
    low = total.astype(BF)
    own_ref[16:32, :] = low[64:80]
    for n in range(NZ):
        step = jnp.bitwise_and(n + NZ - z, NZ - 1)

        @pl.when(step == 0)
        def _():
            own_ref[0:16, :] = low[n * 16 : (n + 1) * 16]

        for k in (1, 2, 3):

            @pl.when(step == k)
            def _():
                sent_refs[k - 1][...] = low[n * 16 : (n + 1) * 16]


def ffn_reduce(where, received):
    return pl.pallas_call(
        ffn_reduce_kernel,
        in_specs=[SM, VM],
        out_specs=[VM] * NZ,
        out_shape=[shape((32, 2 * HID), BF)] + [shape((16, 2 * HID), BF)] * 3,
        compiler_params=params(),
        cost_estimate=cost(0),
        name="ffn_reduce",
    )(where, received)


UP, DOWN, PROJ, QKV, SMALL, WIDE = 0, 2048, 4096, 5120, 6656, 6784


def pack_kernel(where_ref, own_ref, *refs):
    ffn_refs, qkv_ref, out_ref = refs[:3], refs[3], refs[4]
    z = where_ref[1]
    for k in range(NZ):
        ring = jnp.bitwise_and(z + NZ - k, NZ - 1)
        block = own_ref[0:16, :] if k == 0 else ffn_refs[k - 1][...]
        for n in range(8):
            out_ref[n, :, pl.ds(pl.multiple_of(UP + ring * HID, HID), HID)] = block[:, :HID]
            out_ref[n, :, pl.ds(pl.multiple_of(DOWN + ring * HID, HID), HID)] = block[:, HID:]
    small = jnp.zeros((16, 128), F32)
    for ring in range(NZ):
        total = jnp.zeros((16, 4 * PAIR), F32)
        for h in range(NXH):
            for n in range(8):
                total = total + qkv_ref[(h * NZ + ring) * 8 + n].astype(F32)
        small = small + total[:, 3 * PAIR :]
        low = total.astype(BF)
        for n in range(8):
            for part in range(3):
                first = QKV + part * 512 + ring * PAIR
                out_ref[n, :, first : first + PAIR] = low[:, part * PAIR : (part + 1) * PAIR]
    for n in range(8):
        out_ref[n, :, PROJ:QKV] = own_ref[16:32, :]
        out_ref[n, :, SMALL:WIDE] = small.astype(BF)


def pack(where, own, others, qkv):
    return pl.pallas_call(
        pack_kernel,
        in_specs=[SM] + [VM] * 5,
        out_specs=VM,
        out_shape=shape((8, 16, WIDE), BF),
        compiler_params=params(),
        cost_estimate=cost(0),
        name="pack",
    )(where, own, *others, qkv)


def merge_kernel(where_ref, mine_ref, theirs_ref, up_ref, down_ref, proj_ref, qkv_ref, small_ref):
    core = where_ref[0]
    native = where_ref[0] == where_ref[3]
    for side, ref in ((core, mine_ref), (1 - core, theirs_ref)):
        up_ref[:, pl.ds(pl.multiple_of(side * 2048, 2048), 2048)] = ref[:, UP:DOWN]
        down_ref[:, pl.ds(pl.multiple_of(side * 2048, 2048), 2048)] = ref[:, DOWN:PROJ]
        for part in range(3):
            place = pl.multiple_of(part * D + side * 512, 512)
            qkv_ref[:, pl.ds(place, 512)] = ref[:, QKV + part * 512 : QKV + (part + 1) * 512]

    @pl.when(native)
    def _():
        proj_ref[...] = mine_ref[:, PROJ:QKV]

    @pl.when(jnp.logical_not(native))
    def _():
        proj_ref[...] = theirs_ref[:, PROJ:QKV]

    for n in range(8):
        small_ref[2 * n : 2 * n + 2, :] = mine_ref[n * 16 : (n + 1) * 16, SMALL:WIDE].astype(F32)[
            0:2
        ] + theirs_ref[n * 16 : (n + 1) * 16, SMALL:WIDE].astype(F32)[0:2]


def merge(where, mine, theirs):
    return pl.pallas_call(
        merge_kernel,
        in_specs=[SM, VM, VM],
        out_specs=[VM] * 5,
        out_shape=[
            shape((128, FF), BF),
            shape((128, FF), BF),
            shape((128, D), BF),
            shape((128, 3 * D), BF),
            shape((16, 128), F32),
        ],
        compiler_params=params(),
        cost_estimate=cost(0),
        name="merge",
    )(where, mine, theirs)


def back_kernel(dqkv_ref, w_ref, ffn_ref, norm_ref, out_ref):
    dn1 = dot(dqkv_ref[...], w_ref[...], 1, 1)
    out_ref[...] = (dn1 * norm_ref[0:1, :] + ffn_ref[...].astype(F32)).astype(BF)


def back_half(dqkv, w, ffn_back, norms, base):
    moving = lambda i: (base + i, 0)
    fixed = lambda i: (0, 0)
    return pl.pallas_call(
        back_kernel,
        grid=(2,),
        in_specs=[
            pl.BlockSpec((2 * ROWS, 3 * PAIR), moving),
            pl.BlockSpec((D, 3 * PAIR), fixed),
            pl.BlockSpec((2 * ROWS, D), moving),
            pl.BlockSpec((4, D), fixed),
        ],
        out_specs=pl.BlockSpec((2 * ROWS, D), lambda i: (i, 0)),
        out_shape=shape((SEQ // 2, D), BF),
        compiler_params=params(),
        cost_estimate=cost(0),
        name="back_half",
    )(dqkv, w, ffn_back, norms)


def qkv_grad_kernel(meta_ref, xh_ref, dqkv_ref, w_ref, norm_ref, dy_ref, ffn_vec_ref, grad_ref, vec):
    part = meta_ref[6]
    dqkv = dqkv_ref[...]
    sums = jnp.broadcast_to(jnp.sum(dqkv.astype(F32), axis=0, keepdims=True), (8, 3 * PAIR))
    dy_sum = jnp.sum(dy_ref[...].astype(F32), axis=0, keepdims=True)
    raw = dot(xh_ref[...], dqkv, 0, 0)
    gain = jnp.transpose(jnp.broadcast_to(norm_ref[0:1, :], (8, D)))[:, 0:1]
    shift = jnp.transpose(jnp.broadcast_to(norm_ref[1:2, :], (8, D)))[:, 0:1]
    grad_ref[:, 0 : 3 * PAIR] = (raw * gain + shift * sums[0:1, :]).astype(BF)
    product = (raw * w_ref[...].astype(F32)).astype(BF)
    norm_rows = [
        dot(jnp.ones((8, 3 * PAIR), BF), product, 1, 1)[0:1],
        dot(sums.astype(BF), w_ref[...], 1, 1)[0:1],
        ffn_vec_ref[0:1, :],
        ffn_vec_ref[8:9, :],
    ]
    vec[...] = jnp.zeros_like(vec)

    def put(bias_row, values):
        place = bias_row + (bias_row // 9) * 7
        vec[pl.ds(place, 1), :] = values

    for n in range(3):
        put(n * 8 + part, sums[0:1, n * PAIR : (n + 1) * PAIR])
    for n in range(4):
        put(32 + part * 4 + n, ffn_vec_ref[16:17, n * 128 : (n + 1) * 128])
    for n in range(8):
        put(24 + n, dy_sum[:, n * 128 : (n + 1) * 128])
        put(64 + n, dy_sum[:, n * 128 : (n + 1) * 128])
        for r in range(4):
            vec[n * 16 + 9 + r : n * 16 + 10 + r, :] = norm_rows[r][:, n * 128 : (n + 1) * 128]
    grad_ref[:, 3 * PAIR :] = jnp.concatenate(
        [
            part for n in range(64) for part in (vec[2 * n : 2 * n + 2, :], jnp.zeros((14, 128), F32))
        ],
        axis=0,
    ).astype(BF)


def qkv_grad(meta, xh, dqkv, w, norms, dy, ffn_vec):
    return pl.pallas_call(
        qkv_grad_kernel,
        in_specs=[SM] + [VM] * 6,
        out_specs=VM,
        out_shape=shape((D, 4 * PAIR), BF),
        scratch_shapes=[pltpu.VMEM((128, 128), F32)],
        compiler_params=params(),
        cost_estimate=cost(0),
        name="qkv_grad",
    )(meta, xh, dqkv, w, norms, dy, ffn_vec)


def body(
    tokens, out_grad, segments, w_qkv, w_proj, w_up, w_down, norm_params, biases,
    prior_moment_qkv, prior_square_qkv, prior_moment_proj, prior_square_proj,
    prior_moment_up, prior_square_up, prior_moment_down, prior_square_down,
    prior_moment_norm, prior_square_norm, prior_moment_bias, prior_square_bias,
):
    rep, shard = lax.axis_index("rep"), lax.axis_index("shard")
    core, y = rep % NC, rep // (NC * NXL)
    where = jnp.stack([core, shard % NZ, y, shard // NZ]).astype(jnp.int32)

    x_mine = spread([tokens] * NZ)
    docs = segments.astype(BF).reshape(2, 128)
    sent = send_weights(
        where, w_qkv, w_up, w_down, norm_params, biases.reshape(9, 128), docs, sibling(docs)
    )
    received = lax.all_to_all(sent, "shard", 0, 0, tiled=True)
    w_qkv_t, norms, bias, ffn_part, meta = assemble(where, received)
    cosine, sine = rotary_tables()
    x_joined = join(x_mine, 200)
    half = project_qkv(meta, x_joined, w_qkv_t, bias, norms, cosine, sine, None, 100)
    x_other = sibling(x_joined)
    n2, xh, q, k, v = project_qkv(meta, x_other, w_qkv_t, bias, norms, cosine, sine, half, 0)

    ffn_part = exchange(ffn_part, ALONG_Y)
    w_up_t, w_down_t = assemble_ffn(ffn_part)
    dy_first = jnp.concatenate([out_grad, w_proj.astype(BF)], axis=0)
    dy_first, dy_own, _ = lax.optimization_barrier((dy_first, out_grad, x_joined))
    dy_mine = spread([dy_first, dy_own, dy_own, dy_own])

    ctx, ctxt, stat = attn_forward(meta, q, k, v)
    ctx, dy_mine, w_up_t, w_down_t = lax.optimization_barrier((ctx, dy_mine, w_up_t, w_down_t))
    dy_joined = join(dy_mine, 0)
    dy_other = sibling(dy_joined)
    out_mine, out_theirs, ffn_back, dctx, ffn_vec, ffn_sent = feed_forward(
        meta, dy_joined, dy_other, n2, xh, ctx, w_up_t, w_down_t, dy_mine[0], bias, norms
    )
    out_other = sibling(out_theirs)

    prepared = attn_prepare(q, k, dctx, ctxt, stat)
    dqkv = attn_backward(meta, k, v, stat, cosine, sine, prepared)
    qkv_sent = qkv_grad(meta, xh, dqkv, w_qkv_t, norms, out_grad, ffn_vec)
    out_pieces = collect(core_sum(out_mine, out_other))
    dqkv, qkv_sent = lax.optimization_barrier((dqkv, qkv_sent))
    back_theirs = back_half(dqkv, w_qkv_t, ffn_back, norms, 2)
    dqkv, back_theirs, out_pieces = lax.optimization_barrier((dqkv, back_theirs, out_pieces))
    back_mine = back_half(dqkv, w_qkv_t, ffn_back, norms, 0)

    block_out = finish_out(tokens, bias, out_pieces)
    ffn_received, back_mine = lax.optimization_barrier((exchange(ffn_sent, PLANE), back_mine))
    ffn_own, *ffn_others = ffn_reduce(where, ffn_received)
    ffn_others = [lax.ppermute(b, AXES, ROUND_Z[k + 1]) for k, b in enumerate(ffn_others)]
    qkv_rows = exchange(qkv_sent.reshape(64, 16, 4 * PAIR), SAME_CORE)
    back_pieces = collect(core_sum(back_mine, sibling(back_theirs)))
    grad_tokens = finish_grad(tokens, out_grad, back_pieces)
    ffn_own, grad_tokens = lax.optimization_barrier((ffn_own, grad_tokens))
    packed = pack(where, ffn_own, ffn_others, qkv_rows)
    mine_grad = exchange(packed, COPIES).reshape(128, WIDE)
    g_up, g_down, g_proj, g_qkv, small = merge(where, mine_grad, sibling(mine_grad))
    g_norm = small[9:13]
    g_bias = small[:9].reshape(1152)

    def matrix_step(weight, moment, square, grad):
        return adam_step(weight, moment, square, grad.astype(F32), RATE_MATRIX, DECAY)

    new_qkv = matrix_step(w_qkv, prior_moment_qkv, prior_square_qkv, g_qkv)
    new_proj = matrix_step(w_proj, prior_moment_proj, prior_square_proj, g_proj)
    new_up = matrix_step(w_up, prior_moment_up, prior_square_up, g_up)
    new_down = matrix_step(w_down, prior_moment_down, prior_square_down, g_down)
    new_norm = adam_step(norm_params, prior_moment_norm, prior_square_norm, g_norm, RATE_VECTOR, 0.0)
    new_bias = adam_step(biases, prior_moment_bias, prior_square_bias, g_bias, RATE_VECTOR, 0.0)
    return (block_out, grad_tokens, *new_qkv, *new_proj, *new_up, *new_down, *new_norm, *new_bias)


def solution(mesh):
    token = P(("rep", "shard"), None)
    row = P("shard", None)
    norm = P(None, "shard")
    flat = P("shard")
    in_specs = (
        (token, token, P(("rep", "shard")))
        + (row,) * 4
        + (norm, flat)
        + (row,) * 8
        + (norm, norm, flat, flat)
    )
    out_specs = (token, token) + (row,) * 12 + (norm,) * 3 + (flat,) * 3
    return jax.shard_map(body, mesh=mesh, in_specs=in_specs, out_specs=out_specs, check_vma=False)
```

time: 1500 us -> 305 us (0.20)
  waiting for transfers between devices: 1030 us -> 52.6 us
  matrix products: 176 us -> 0 us
  blocking collectives: 152 us -> 27.1 us
  Pallas kernels: 0 us -> 95.1 us
  other arithmetic: 97.9 us -> 15.2 us
  starting transfers between devices: 0.59 us -> 81.1 us
    reduce_scatter x2 -> x0, waiting for transfers between devices: 609 us -> none  [the longest x1 470 us: body(): lax.psum_scatter(jnp.concatenate([contract_rows(normed_one, grad_qkv), co...]
    all_gather x6 -> x0, waiting for transfers between devices: 287 us -> none  [the longest x1 95.3 us: body(): lax.all_gather(w_down.astype(jnp.bfloat16), 'shard', axis=0, tiled=True)]
    dot_general x18 -> x0, matrix products: 176 us -> none  [the longest x4 27.2 us: contract_rows(): lax.dot_general(left, right, (((0,), (0,)), ((), ())), preferred_element_...]
    psum x1 -> x0, waiting for transfers between devices: 101 us -> none  [body(): lax.psum((matrix_grad, norm_part, bias_part), 'rep')]
    pallas_call x0 -> x21, Pallas kernels: none -> 95.1 us  [the longest x1 22.9 us: feed_forward(): pl.pallas_call(ffn_kernel, grid_spec=pltpu.PrefetchScalarGridSpec(num_sca...]
    all_gather x3 -> x0, blocking collectives: 64.7 us -> none  [the longest x1 30 us: body(): lax.all_gather(biases.astype(jnp.bfloat16), 'shard', axis=0, tiled=True)]
    ppermute x0 -> x25, starting transfers between devices: none -> 57.4 us  [the longest x8 24.3 us: collect(): return [lax.ppermute(b, AXES, COLLECT[k]) for k, b in enumerate(blocks)]]
    psum x1 -> x0, blocking collectives: 53.4 us -> none  [body(): lax.psum((matrix_grad, norm_part, bias_part), 'rep')]
  transfers between devices with their start and end apart: 10 -> 29, of which waited for: 9 -> 12; matrix products, arithmetic and copies ran while one was open for 16% -> 1% of each run, Pallas kernels for 0% -> 23%
where the time goes in v1:
time: 305 us; the launch traced here: 303 us
  Pallas kernels  95.1 us (31%)
  starting transfers between devices  81.1 us (27%)
  waiting for transfers between devices  52.6 us (17%)
  local copies, waits for them, and re-layouts  30.5 us (10%)
  blocking collectives  27.1 us (9%)
  other arithmetic  15.2 us (5%)
    ppermute x8, waiting for transfers between devices, collect(): return [lax.ppermute(b, AXES, COLLECT[k]) for k, b in enumerate(blocks)]  34.2 us
    unnamed x130, local copies, waits for them, and re-layouts  30.5 us
    all_to_all x1, blocking collectives, exchange(): lax.all_to_all(values, AXES, 0, 0, axis_index_groups=members, tiled=True)  27.1 us
    ppermute x8, starting transfers between devices, collect(): return [lax.ppermute(b, AXES, COLLECT[k]) for k, b in enumerate(blocks)]  24.3 us
    ppermute x8, starting transfers between devices, spread(): return [lax.ppermute(b, AXES, SPREAD[k]) for k, b in enumerate(blocks)]  23.3 us
    pallas_call x1, Pallas kernels, feed_forward(): pl.pallas_call(ffn_kernel, grid_spec=pltpu.PrefetchScalarGridSpec(num_sca...  22.9 us
    pallas_call x1, Pallas kernels, attn_backward(): pl.pallas_call(attn_backward_kernel, grid=(SEQ // QB,), in_specs=[SM] + [...  19.4 us
    all_to_all x3, starting transfers between devices, exchange(): lax.all_to_all(values, AXES, 0, 0, axis_index_groups=members, tiled=True)  17.7 us
  transfers between devices with their start and end apart: 29, of which 12 were waited for; matrix products, arithmetic and copies ran while one was open for 1% of the time, Pallas kernels for 23%

profile of v1, /device:TPU:1, one launch (start us, length us, event | category | flops | bytes accessed | tf_op | source)
XLA Modules:
  0.0 303.1 jit_solution(11451931782690115111)
XLA Ops:
  0.7 7.7 %collective-permute-start.4 = (bf16[256,1024]{1,0:T(8,128)(2,1)}, bf16[256,1024]{1,0:T(8,128)(2,1)S(1)}, u32[]{:S(2)}, u32[]{:S(2)}) collective-permute-start(bf16[256,1024]{1,0:T(8,128)(2,1)} %x_ref.3), channel_id=1, source_target_pairs={{0,3},{1,0},{2,1},{3,2},{4,11},{5,8},{6,9},{7,10},{8,7},{9,4},{10,... | collective-permute-start | bytes 1572872 | tf_op jit(solution)/shard_map/ppermute | solution.py:97
  8.4 3.4 %collective-permute-start.2 = (bf16[256,1024]{1,0:T(8,128)(2,1)}, bf16[256,1024]{1,0:T(8,128)(2,1)}, u32[]{:S(2)}, u32[]{:S(2)}) collective-permute-start(bf16[256,1024]{1,0:T(8,128)(2,1)} %x_ref.3), channel_id=1, source_target_pairs={{0,1},{1,2},{2,3},{3,0},{4,9},{5,10},{6,11},{7,8},{8,5},{9,6},{10,... | collective-permute-start | bytes 1572872 | tf_op jit(solution)/shard_map/ppermute | solution.py:97
  11.8 2.2 collective-permute-start.1
  15.7 2.0 pad_maximum_fusion
  22.8 6.0 %all-to-all-start = ((bf16[8,240,384]{2,1,0:T(8,128)(2,1)}), bf16[8,240,384]{2,1,0:T(8,128)(2,1)S(1)}, u32[]{:S(2)}, u32[]{:S(2)}) async-start(bf16[8,240,384]{2,1,0:T(8,128)(2,1)} %copy-done.13), calls=%async_computation | async-start | bytes 2949120 | tf_op jit(solution)/shard_map/all_to_all | solution.py:953
  29.3 10.4 %collective-permute-done.1.refs_0_ = bf16[256,1024]{1,0:T(8,128)(2,1)} collective-permute-done((bf16[256,1024]{1,0:T(8,128)(2,1)}, bf16[256,1024]{1,0:T(8,128)(2,1)}, u32[]{:S(2)}, u32[]{:S(2)}) %collective-permute-start.1) | collective-permute-done | bytes 524320 | tf_op jit(solution)/shard_map/ppermute | solution.py:97
  39.7 2.7 join.2.x_ref
  42.4 1.9 collective-permute-start.8
  44.2 2.3 collective-permute-start.7
  46.5 5.9 %collective-permute-start.6 = (bf16[384,1024]{1,0:T(8,128)(2,1)}, bf16[384,1024]{1,0:T(8,128)(2,1)}, u32[]{:S(2)}, u32[]{:S(2)}) collective-permute-start(bf16[384,1024]{1,0:T(8,128)(2,1)} %pad_maximum_fusion), channel_id=1, source_target_pairs={{0,0},{1,1},{2,2},{3,3},{4,8},{5,9},{6,10},{7,11},{8,4},{9,5},{10,... | collective-permute-start | bytes 2359304 | tf_op jit(solution)/shard_map/ppermute | solution.py:97
  55.5 4.2 %all-to-all-start.1 = ((bf16[4,256,1024]{2,1,0:T(8,128)(2,1)}), bf16[4,256,1024]{2,1,0:T(8,128)(2,1)S(1)}, u32[]{:S(2)}, u32[]{:S(2)}) async-start(bf16[4,256,1024]{2,1,0:T(8,128)(2,1)} %copy-done.25), calls=%async_computation.1 | async-start | bytes 4194304 | tf_op jit(solution)/shard_map/all_to_all | solution.py:109
  62.1 5.3 %project_qkv.2 = (bf16[2048,1024]{1,0:T(8,128)(2,1)S(1)}, bf16[2048,1024]{1,0:T(8,128)(2,1)S(1)}, bf16[2048,128]{1,0:T(8,128)(2,1)S(1)}, bf16[2048,128]{1,0:T(8,128)(2,1)S(1)}, bf16[2048,128]{1,0:T(8,128)(2,1)S(1)}) custom-call(s32[24]{0:T(128)S(1)} %get-tuple-element.90.meta_ref, bf16[1024,1024]{1,0:T(8,128)(2,1)} %join.2.x_ref, ...), custom_call_target="tpu_custom_call" | custom-call | flops 70000001024 | bytes 200000000 | tf_op jit(solution)/shard_map/project_qkv/pallas_call | solution.py:333
  67.5 5.4 %project_qkv.3 = (bf16[2048,1024]{1,0:T(8,128)(2,1)S(1)}, bf16[2048,1024]{1,0:T(8,128)(2,1)S(1)}, bf16[2048,128]{1,0:T(8,128)(2,1)S(1)}, bf16[2048,128]{1,0:T(8,128)(2,1)S(1)}, bf16[2048,128]{1,0:T(8,128)(2,1)S(1)}) custom-call(s32[24]{0:T(128)S(1)} %get-tuple-element.90.meta_ref, ...), custom_call_target="tpu_custom_call", output_to_operand_aliasing={{0}: (7, {}), {1}: (8, {}), {2}: (9, {}), {3}: (10, {}), {4... | custom-call | tf_op jit(solution)/shard_map/project_qkv/pallas_call | solution.py:333
  72.9 2.0 copy-done.3
  74.9 2.0 copy-done.15
  76.9 14.8 %attn_forward.1 = (bf16[2048,128]{1,0:T(8,128)(2,1)S(1)}, f32[128,2048]{1,0:T(8,128)S(1)}, f32[8,2048]{1,0:T(8,128)S(1)}) custom-call(s32[24]{0:T(128)S(1)} %get-tuple-element.90.meta_ref, bf16[2048,128]{1,0:T(8,128)(2,1)S(1)} %get-tuple-element.100.q_ref, bf16[2048,128]{1,0:T(8,128)(2,1)S(1)} %get-tuple-element.98.k_ref, ...), custom_call_target="tpu_custom_call" | custom-call | tf_op jit(solution)/shard_map/attn_forward/pallas_call | solution.py:421
  97.0 2.5 collective-permute-start.10
  99.5 3.8 %collective-permute-done.10.refs_1_ = bf16[1024,1024]{1,0:T(8,128)(2,1)S(1)} collective-permute-done((bf16[1024,1024]{1,0:T(8,128)(2,1)S(1)}, bf16[1024,1024]{1,0:T(8,128)(2,1)S(1)}, u32[]{:S(2)}, u32[]{:S(2)}) %collective-permute-start.10) | collective-permute-done | bytes 2097184 | tf_op jit(solution)/shard_map/ppermute | solution.py:105
  103.3 22.9 %feed_forward.1 = (bf16[1024,1024]{1,0:T(8,128)(2,1)S(1)}, bf16[1024,1024]{1,0:T(8,128)(2,1)S(1)}, bf16[2048,1024]{1,0:T(8,128)(2,1)S(1)}, f32[2048,128]{1,0:T(8...) custom-call(s32[24]{0:T(128)S(1)} %get-tuple-element.90.meta_ref, bf16[1024,1024]{1,0:T(8,128)(2,1)S(1)} %join.3.refs_0_, ...), custom_call_target="tpu_custom_call" | custom-call | flops 41999998976 | bytes 120000000 | tf_op jit(solution)/shard_map/feed_forward/pallas_call | solution.py:632
  126.2 2.0 copy-done
  132.5 8.0 %all-to-all-start.2 = ((bf16[16,80,1024]{2,1,0:T(8,128)(2,1)}), bf16[16,80,1024]{2,1,0:T(8,128)(2,1)}, u32[]{:S(2)}, u32[]{:S(2)}) async-start(bf16[16,80,1024]{2,1,0:T(8,128)(2,1)} %get-tuple-element.137), calls=%async_computation.2 | async-start | bytes 5242880 | tf_op jit(solution)/shard_map/all_to_all | solution.py:109
  146.2 5.2 %collective-permute-start.12 = (bf16[256,1024]{1,0:T(8,128)(2,1)S(1)}, bf16[256,1024]{1,0:T(8,128)(2,1)S(1)}, u32[]{:S(2)}, u32[]{:S(2)}) collective-permute-start(bf16[256,1024]{1,0:T(8,128)(2,1)S(1)} %get-tuple-element.129), channel_id=1, source_target_pairs={{0,0},{1,1},{2,2},{3,3},{8,4},{9,5},{10,6},{11,7},{4,8},{5,9},{6,1... | collective-permute-start | bytes 1572872 | tf_op jit(solution)/shard_map/ppermute | solution.py:101
  151.4 2.2 collective-permute-start.13
  153.5 3.5 %collective-permute-start.14 = (bf16[256,1024]{1,0:T(8,128)(2,1)S(1)}, bf16[256,1024]{1,0:T(8,128)(2,1)S(1)}, u32[]{:S(2)}, u32[]{:S(2)}) collective-permute-start(bf16[256,1024]{1,0:T(8,128)(2,1)S(1)} %get-tuple-element.131), channel_id=1, source_target_pairs={{2,0},{3,1},{0,2},{1,3},{10,4},{11,5},{8,6},{9,7},{6,8},{7,9},{4,1... | collective-permute-start | bytes 1572872 | tf_op jit(solution)/shard_map/ppermute | solution.py:101
  157.1 2.0 collective-permute-start.15
  159.1 19.4 %attn_backward.1.dqkv_ref = bf16[2048,384]{1,0:T(8,128)(2,1)S(1)} custom-call(s32[24]{0:T(128)S(1)} %get-tuple-element.90.meta_ref, bf16[2048,128]{1,0:T(8,128)(2,1)S(1)} %copy-done.20, bf16[2048,128]{1,0:T(8,128)(2,1)S(1)} %copy-done.22, f32[8,2048]{1,0:T(8,128)S(1)} %get-tuple-element.101.stat_ref, f32[2048,128]{1,0:T(8,128)S(1)} %copy-done.30, ...), custom_call_target="tpu_custom_call" | custom-call | flops 70000001024 | bytes 200000000 | tf_op jit(solution)/shard_map/attn_backward/pallas_call | solution.py:524
  178.6 3.5 %qkv_grad.1 = bf16[1024,512]{1,0:T(8,128)(2,1)S(1)} custom-call(s32[24]{0:T(128)S(1)} %get-tuple-element.90.meta_ref, bf16[2048,1024]{1,0:T(8,128)(2,1)S(1)} %copy-done.4, bf16[2048,384]{1,0:T(8,128)(2,1)S(1)} %attn_backward.1.dqkv_ref, bf16[1024,384]{1,0:T(8,128)(2,1)S(1)} %copy-done.6, f32[4,1024]{1,0:T(4,128)S(1)} %get-tuple-element.92.norm_ref.refs_9_, ...), custom_call_target="tpu_custom_call" | custom-call | tf_op jit(solution)/shard_map/qkv_grad/pallas_call | solution.py:926
  182.1 2.5 back_half.2
  184.6 2.0 collective-permute-done.12.refs_0_
  187.5 5.7 %collective-permute-done.13.refs_1_ = bf16[256,1024]{1,0:T(8,128)(2,1)S(1)} collective-permute-done((bf16[256,1024]{1,0:T(8,128)(2,1)S(1)}, bf16[256,1024]{1,0:T(8,128)(2,1)S(1)}, u32[]{:S(2)}, u32[]{:S(2)}) %collective-permute-start.13) | collective-permute-done | bytes 524320 | tf_op jit(solution)/shard_map/ppermute | solution.py:101
  194.0 8.7 %collective-permute-done.14.refs_2_ = bf16[256,1024]{1,0:T(8,128)(2,1)S(1)} collective-permute-done((bf16[256,1024]{1,0:T(8,128)(2,1)S(1)}, bf16[256,1024]{1,0:T(8,128)(2,1)S(1)}, u32[]{:S(2)}, u32[]{:S(2)}) %collective-permute-start.14) | collective-permute-done | bytes 524320 | tf_op jit(solution)/shard_map/ppermute | solution.py:101
  203.5 3.8 %collective-permute-done.15.refs_3_ = bf16[256,1024]{1,0:T(8,128)(2,1)S(1)} collective-permute-done((bf16[256,1024]{1,0:T(8,128)(2,1)S(1)}, bf16[256,1024]{1,0:T(8,128)(2,1)S(1)}, u32[]{:S(2)}, u32[]{:S(2)}) %collective-permute-start.15) | collective-permute-done | bytes 524320 | tf_op jit(solution)/shard_map/ppermute | solution.py:101
  208.1 5.5 %all-to-all-start.3 = ((bf16[64,16,512]{2,1,0:T(8,128)(2,1)}), bf16[64,16,512]{2,1,0:T(8,128)(2,1)}, u32[]{:S(2)}, u32[]{:S(2)}) async-start(bf16[64,16,512]{2,1,0:T(8,128)(2,1)} %bitcast.18), calls=%async_computation.3 | async-start | bytes 2097152 | tf_op jit(solution)/shard_map/all_to_all | solution.py:109
  213.6 2.2 copy-done.2
  217.3 3.0 core_sum.3
  220.3 5.3 %collective-permute-start.17 = (bf16[256,1024]{1,0:T(8,128)(2,1)S(1)}, bf16[256,1024]{1,0:T(8,128)(2,1)S(1)}, u32[]{:S(2)}, u32[]{:S(2)}) collective-permute-start(bf16[256,1024]{1,0:T(8,128)(2,1)S(1)} %get-tuple-element.143), channel_id=1, source_target_pairs={{0,0},{1,1},{2,2},{3,3},{8,4},{9,5},{10,6},{11,7},{4,8},{5,9},{6,1... | collective-permute-start | bytes 1572872 | tf_op jit(solution)/shard_map/ppermute | solution.py:101
  225.6 2.4 collective-permute-start.18
  227.9 3.4 %collective-permute-start.19 = (bf16[256,1024]{1,0:T(8,128)(2,1)S(1)}, bf16[256,1024]{1,0:T(8,128)(2,1)S(1)}, u32[]{:S(2)}, u32[]{:S(2)}) collective-permute-start(bf16[256,1024]{1,0:T(8,128)(2,1)S(1)} %get-tuple-element.145), channel_id=1, source_target_pairs={{2,0},{3,1},{0,2},{1,3},{10,4},{11,5},{8,6},{9,7},{6,8},{7,9},{4,1... | collective-permute-start | bytes 1572872 | tf_op jit(solution)/shard_map/ppermute | solution.py:101
  231.7 2.2 ffn_reduce.1
  237.4 2.8 collective-permute-done.18.refs_1_
  240.2 2.5 collective-permute-start.23
  242.7 6.6 %collective-permute-done.19.refs_2_ = bf16[256,1024]{1,0:T(8,128)(2,1)S(1)} collective-permute-done((bf16[256,1024]{1,0:T(8,128)(2,1)S(1)}, bf16[256,1024]{1,0:T(8,128)(2,1)S(1)}, u32[]{:S(2)}, u32[]{:S(2)}) %collective-permute-start.19) | collective-permute-done | bytes 524320 | tf_op jit(solution)/shard_map/ppermute | solution.py:101
  249.3 4.6 %collective-permute-done.20.refs_3_ = bf16[256,1024]{1,0:T(8,128)(2,1)S(1)} collective-permute-done((bf16[256,1024]{1,0:T(8,128)(2,1)S(1)}, bf16[256,1024]{1,0:T(8,128)(2,1)S(1)}, u32[]{:S(2)}, u32[]{:S(2)}) %collective-permute-start.20) | collective-permute-done | bytes 524320 | tf_op jit(solution)/shard_map/ppermute | solution.py:101
  253.9 1.8 finish_grad.1
  257.3 27.1 %all_to_all.25 = bf16[8,16,6784]{2,1,0:T(8,128)(2,1)S(1)} all-to-all(bf16[8,16,6784]{2,1,0:T(8,128)(2,1)S(1)} %pack.1), channel_id=1, replica_groups={{0,16,32,48,64,80,96,112},{1,17,33,49,65,81,97,113},{2,18,34,50,66,82,9..., dimensions={0} | all-to-all | bytes 3473408 | tf_op jit(solution)/shard_map/all_to_all | solution.py:109
  286.5 2.0 collective-permute-done.24.theirs_ref
  292.1 3.1 %multiply_subtract_fusion.2 = (f32[128,3072]{1,0:T(8,128)}, f32[128,3072]{1,0:T(8,128)}, f32[128,3072]{1,0:T(8,128)}) fusion(f32[128,3072]{1,0:T(8,128)S(1)} %copy-done.12, bf16[128,3072]{1,0:T(8,128)(2,1)S(1)} %get-tuple-element.153, f32[128,3072]{1,0:T(8,128)S(1)} %copy-done.57, f32[128,3072]{1,0:T(8,128)S(1)} %copy-done.58), kind=kLoop, calls=%fused_computation.14 | loop fusion | flops 6291456 | bytes 10223616 | tf_op jit(solution)/shard_map/sub | solution.py:127
  297.3 5.7 %multiply_subtract_fusion = (f32[128,4096]{1,0:T(8,128)}, f32[128,4096]{1,0:T(8,128)}, f32[128,4096]{1,0:T(8,128)}, f32[128,4096]{1,0:T(8,128)}, f32[128,4096]{1,0:T(8,128)}, /*index=5*/f32[128,4096]{1,0:T(8,128)}) fusion(f32[128,4096]{1,0:T(8,128)S(1)} %copy-done.10, bf16[128,4096]{1,0:T(8,128)(2,1)S(1)} %get-tuple-element.156, ...), kind=kLoop, calls=%fused_computation.9 | loop fusion | flops 16777216 | bytes 27262976 | tf_op jit(solution)/shard_map/sub | solution.py:127
  (171 shorter events, 45.6 us)
Async XLA Ops:
  0.7 17.1 %copy-start.45 = (f32[4,128]{1,0:T(4,128)S(1)}, f32[4,128]{1,0:T(4,128)}, u32[]{:S(2)}) copy-start(f32[4,128]{1,0:T(4,128)} %norm_ref.1) | copy-start | bytes 6148
  0.7 17.1 %copy-start.7 = (f32[128,4096]{1,0:T(8,128)S(1)}, f32[128,4096]{1,0:T(8,128)}, u32[]{:S(2)}) copy-start(f32[128,4096]{1,0:T(8,128)} %up_ref.1) | copy-start | bytes 6291460
  0.7 17.1 %copy-start.41 = (f32[1152]{0:T(1024)S(1)}, f32[1152]{0:T(1024)}, u32[]{:S(2)}) copy-start(f32[1152]{0:T(1024)} %param.31) | copy-start | bytes 13828
  0.7 28.2 %collective-permute-start.4 = (bf16[256,1024]{1,0:T(8,128)(2,1)}, bf16[256,1024]{1,0:T(8,128)(2,1)S(1)}, u32[]{:S(2)}, u32[]{:S(2)}) collective-permute-start(bf16[256,1024]{1,0:T(8,128)(2,1)} %x_ref.3), channel_id=1, source_target_pairs={{0,3},{1,0},{2,1},{3,2},{4,11},{5,8},{6,9},{7,10},{8,7},{9,4},{10,... | collective-permute-start | bytes 1572872 | tf_op jit(solution)/shard_map/ppermute | solution.py:97
  8.4 20.5 %collective-permute-start.3 = (bf16[256,1024]{1,0:T(8,128)(2,1)}, bf16[256,1024]{1,0:T(8,128)(2,1)S(1)}, u32[]{:S(2)}, u32[]{:S(2)}) collective-permute-start(bf16[256,1024]{1,0:T(8,128)(2,1)} %x_ref.3), channel_id=1, source_target_pairs={{0,2},{1,3},{2,0},{3,1},{4,10},{5,11},{6,8},{7,9},{8,6},{9,7},{10,... | collective-permute-start | bytes 1572872 | tf_op jit(solution)/shard_map/ppermute | solution.py:97
  8.4 21.0 %collective-permute-start.2 = (bf16[256,1024]{1,0:T(8,128)(2,1)}, bf16[256,1024]{1,0:T(8,128)(2,1)}, u32[]{:S(2)}, u32[]{:S(2)}) collective-permute-start(bf16[256,1024]{1,0:T(8,128)(2,1)} %x_ref.3), channel_id=1, source_target_pairs={{0,1},{1,2},{2,3},{3,0},{4,9},{5,10},{6,11},{7,8},{8,5},{9,6},{10,... | collective-permute-start | bytes 1572872 | tf_op jit(solution)/shard_map/ppermute | solution.py:97
  11.8 27.9 %collective-permute-start.1 = (bf16[256,1024]{1,0:T(8,128)(2,1)}, bf16[256,1024]{1,0:T(8,128)(2,1)}, u32[]{:S(2)}, u32[]{:S(2)}) collective-permute-start(bf16[256,1024]{1,0:T(8,128)(2,1)} %x_ref.3), channel_id=1, source_target_pairs={{0,0},{1,1},{2,2},{3,3},{4,8},{5,9},{6,10},{7,11},{8,4},{9,5},{10,... | collective-permute-start | bytes 1572872 | tf_op jit(solution)/shard_map/ppermute | solution.py:97
  14.6 3.2 %collective-permute-start = (bf16[2,128]{1,0:T(2,128)(2,1)S(1)}, bf16[2,128]{1,0:T(2,128)(2,1)S(1)}, u32[]{:S(2)}, u32[]{:S(2)}) collective-permute-start(bf16[2,128]{1,0:T(2,128)(2,1)S(1)} %convert_bitcast_fusion.seg_ref), channel_id=1, source_target_pairs={{0,8},{1,9},{2,10},{3,11},{4,12},{5,13},{6,14},{7,15},{8,0},{9,1},... | collective-permute-start | bytes 1544 | tf_op jit(solution)/shard_map/ppermute | solution.py:105
  17.8 34.7 %copy-start.43 = (s32[4]{0:T(128)}, s32[4]{0:T(128)S(1)}, u32[]{:S(2)}) copy-start(s32[4]{0:T(128)S(1)} %pad_add_fusion.where_ref) | copy-start | bytes 52
  22.8 29.7 %all-to-all-start = ((bf16[8,240,384]{2,1,0:T(8,128)(2,1)}), bf16[8,240,384]{2,1,0:T(8,128)(2,1)S(1)}, u32[]{:S(2)}, u32[]{:S(2)}) async-start(bf16[8,240,384]{2,1,0:T(8,128)(2,1)} %copy-done.13), calls=%async_computation | async-start | bytes 2949120 | tf_op jit(solution)/shard_map/all_to_all | solution.py:953
  28.8 13.5 %copy-start.14 = (bf16[256,1024]{1,0:T(8,128)(2,1)S(1)}, bf16[256,1024]{1,0:T(8,128)(2,1)}, u32[]{:S(2)}) copy-start(bf16[256,1024]{1,0:T(8,128)(2,1)} %dy_ref.3) | copy-start | bytes 1572868
  42.4 52.8 %collective-permute-start.9 = (bf16[256,1024]{1,0:T(8,128)(2,1)S(1)}, bf16[256,1024]{1,0:T(8,128)(2,1)}, u32[]{:S(2)}, u32[]{:S(2)}) collective-permute-start(bf16[256,1024]{1,0:T(8,128)(2,1)S(1)} %copy-done.14), channel_id=1, source_target_pairs={{0,3},{1,0},{2,1},{3,2},{4,11},{5,8},{6,9},{7,10},{8,7},{9,4},{10,... | collective-permute-start | bytes 1572872 | tf_op jit(solution)/shard_map/ppermute | solution.py:97
  42.4 52.8 %collective-permute-start.8 = (bf16[256,1024]{1,0:T(8,128)(2,1)S(1)}, bf16[256,1024]{1,0:T(8,128)(2,1)}, u32[]{:S(2)}, u32[]{:S(2)}) collective-permute-start(bf16[256,1024]{1,0:T(8,128)(2,1)S(1)} %copy-done.14), channel_id=1, source_target_pairs={{0,2},{1,3},{2,0},{3,1},{4,10},{5,11},{6,8},{7,9},{8,6},{9,7},{10,... | collective-permute-start | bytes 1572872 | tf_op jit(solution)/shard_map/ppermute | solution.py:97
  44.2 51.0 %collective-permute-start.7 = (bf16[256,1024]{1,0:T(8,128)(2,1)S(1)}, bf16[256,1024]{1,0:T(8,128)(2,1)}, u32[]{:S(2)}, u32[]{:S(2)}) collective-permute-start(bf16[256,1024]{1,0:T(8,128)(2,1)S(1)} %copy-done.14), channel_id=1, source_target_pairs={{0,1},{1,2},{2,3},{3,0},{4,9},{5,10},{6,11},{7,8},{8,5},{9,6},{10,... | collective-permute-start | bytes 1572872 | tf_op jit(solution)/shard_map/ppermute | solution.py:97
  46.5 21.0 %collective-permute-start.5 = (bf16[1024,1024]{1,0:T(8,128)(2,1)}, bf16[1024,1024]{1,0:T(8,128)(2,1)}, u32[]{:S(2)}, u32[]{:S(2)}) collective-permute-start(bf16[1024,1024]{1,0:T(8,128)(2,1)} %join.2.x_ref), channel_id=1, source_target_pairs={{0,8},{1,9},{2,10},{3,11},{4,12},{5,13},{6,14},{7,15},{8,0},{9,1},... | collective-permute-start | bytes 6291464 | tf_op jit(solution)/shard_map/ppermute | solution.py:105
  46.5 48.7 %collective-permute-start.6 = (bf16[384,1024]{1,0:T(8,128)(2,1)}, bf16[384,1024]{1,0:T(8,128)(2,1)}, u32[]{:S(2)}, u32[]{:S(2)}) collective-permute-start(bf16[384,1024]{1,0:T(8,128)(2,1)} %pad_maximum_fusion), channel_id=1, source_target_pairs={{0,0},{1,1},{2,2},{3,3},{4,8},{5,9},{6,10},{7,11},{8,4},{9,5},{10,... | collective-permute-start | bytes 2359304 | tf_op jit(solution)/shard_map/ppermute | solution.py:97
  55.5 12.0 %copy-start.5 = (bf16[1024,384]{1,0:T(8,128)(2,1)}, bf16[1024,384]{1,0:T(8,128)(2,1)S(1)}, u32[]{:S(2)}) copy-start(bf16[1024,384]{1,0:T(8,128)(2,1)S(1)} %get-tuple-element.91.w_ref) | copy-start | bytes 2359300
  55.5 39.6 %all-to-all-start.1 = ((bf16[4,256,1024]{2,1,0:T(8,128)(2,1)}), bf16[4,256,1024]{2,1,0:T(8,128)(2,1)S(1)}, u32[]{:S(2)}, u32[]{:S(2)}) async-start(bf16[4,256,1024]{2,1,0:T(8,128)(2,1)} %copy-done.25), calls=%async_computation.1 | async-start | bytes 4194304 | tf_op jit(solution)/shard_map/all_to_all | solution.py:109
  97.0 6.3 %collective-permute-start.10 = (bf16[1024,1024]{1,0:T(8,128)(2,1)S(1)}, bf16[1024,1024]{1,0:T(8,128)(2,1)S(1)}, u32[]{:S(2)}, u32[]{:S(2)}) collective-permute-start(bf16[1024,1024]{1,0:T(8,128)(2,1)S(1)} %join.3.refs_0_), channel_id=1, source_target_pairs={{0,8},{1,9},{2,10},{3,11},{4,12},{5,13},{6,14},{7,15},{8,0},{9,1},... | collective-permute-start | bytes 6291464 | tf_op jit(solution)/shard_map/ppermute | solution.py:105
  132.5 8.5 %copy-start.49 = (f32[128,2048]{1,0:T(8,128)S(1)}, f32[128,2048]{1,0:T(8,128)}, u32[]{:S(2)}) copy-start(f32[128,2048]{1,0:T(8,128)} %copy-done.48) | copy-start | bytes 3145732
  132.5 75.6 %all-to-all-start.2 = ((bf16[16,80,1024]{2,1,0:T(8,128)(2,1)}), bf16[16,80,1024]{2,1,0:T(8,128)(2,1)}, u32[]{:S(2)}, u32[]{:S(2)}) async-start(bf16[16,80,1024]{2,1,0:T(8,128)(2,1)} %get-tuple-element.137), calls=%async_computation.2 | async-start | bytes 5242880 | tf_op jit(solution)/shard_map/all_to_all | solution.py:109
  140.5 4.5 %collective-permute-start.11 = (bf16[1024,1024]{1,0:T(8,128)(2,1)}, bf16[1024,1024]{1,0:T(8,128)(2,1)S(1)}, u32[]{:S(2)}, u32[]{:S(2)}) collective-permute-start(bf16[1024,1024]{1,0:T(8,128)(2,1)} %copy-done.47), channel_id=1, source_target_pairs={{0,8},{1,9},{2,10},{3,11},{4,12},{5,13},{6,14},{7,15},{8,0},{9,1},... | collective-permute-start | bytes 6291464 | tf_op jit(solution)/shard_map/ppermute | solution.py:105
  145.0 14.1 %copy-start.22 = (bf16[2048,128]{1,0:T(8,128)(2,1)S(1)}, bf16[2048,128]{1,0:T(8,128)(2,1)}, u32[]{:S(2)}) copy-start(bf16[2048,128]{1,0:T(8,128)(2,1)} %copy-done.21) | copy-start | bytes 1572868
  145.0 14.1 %copy-start.28 = (f32[2048,128]{1,0:T(8,128)S(1)}, f32[2048,128]{1,0:T(8,128)}, u32[]{:S(2)}) copy-start(f32[2048,128]{1,0:T(8,128)} %constant.119.clone.sin_ref) | copy-start | bytes 3145732
  145.0 14.1 %copy-start.30 = (f32[2048,128]{1,0:T(8,128)S(1)}, f32[2048,128]{1,0:T(8,128)}, u32[]{:S(2)}) copy-start(f32[2048,128]{1,0:T(8,128)} %constant.118.clone.cos_ref) | copy-start | bytes 3145732
  146.2 40.5 %collective-permute-start.12 = (bf16[256,1024]{1,0:T(8,128)(2,1)S(1)}, bf16[256,1024]{1,0:T(8,128)(2,1)S(1)}, u32[]{:S(2)}, u32[]{:S(2)}) collective-permute-start(bf16[256,1024]{1,0:T(8,128)(2,1)S(1)} %get-tuple-element.129), channel_id=1, source_target_pairs={{0,0},{1,1},{2,2},{3,3},{8,4},{9,5},{10,6},{11,7},{4,8},{5,9},{6,1... | collective-permute-start | bytes 1572872 | tf_op jit(solution)/shard_map/ppermute | solution.py:101
  151.4 41.8 %collective-permute-start.13 = (bf16[256,1024]{1,0:T(8,128)(2,1)S(1)}, bf16[256,1024]{1,0:T(8,128)(2,1)S(1)}, u32[]{:S(2)}, u32[]{:S(2)}) collective-permute-start(bf16[256,1024]{1,0:T(8,128)(2,1)S(1)} %get-tuple-element.130), channel_id=1, source_target_pairs={{1,0},{2,1},{3,2},{0,3},{9,4},{10,5},{11,6},{8,7},{5,8},{6,9},{7,1... | collective-permute-start | bytes 1572872 | tf_op jit(solution)/shard_map/ppermute | solution.py:101
  153.5 49.1 %collective-permute-start.14 = (bf16[256,1024]{1,0:T(8,128)(2,1)S(1)}, bf16[256,1024]{1,0:T(8,128)(2,1)S(1)}, u32[]{:S(2)}, u32[]{:S(2)}) collective-permute-start(bf16[256,1024]{1,0:T(8,128)(2,1)S(1)} %get-tuple-element.131), channel_id=1, source_target_pairs={{2,0},{3,1},{0,2},{1,3},{10,4},{11,5},{8,6},{9,7},{6,8},{7,9},{4,1... | collective-permute-start | bytes 1572872 | tf_op jit(solution)/shard_map/ppermute | solution.py:101
  157.1 50.2 %collective-permute-start.15 = (bf16[256,1024]{1,0:T(8,128)(2,1)S(1)}, bf16[256,1024]{1,0:T(8,128)(2,1)S(1)}, u32[]{:S(2)}, u32[]{:S(2)}) collective-permute-start(bf16[256,1024]{1,0:T(8,128)(2,1)S(1)} %get-tuple-element.132), channel_id=1, source_target_pairs={{3,0},{0,1},{1,2},{2,3},{11,4},{8,5},{9,6},{10,7},{7,8},{4,9},{5,1... | collective-permute-start | bytes 1572872 | tf_op jit(solution)/shard_map/ppermute | solution.py:101
  159.1 19.5 %copy-start.4 = (bf16[2048,1024]{1,0:T(8,128)(2,1)S(1)}, bf16[2048,1024]{1,0:T(8,128)(2,1)}, u32[]{:S(2)}) copy-start(bf16[2048,1024]{1,0:T(8,128)(2,1)} %copy-done.3) | copy-start | bytes 12582916
  159.1 19.5 %copy-start.6 = (bf16[1024,384]{1,0:T(8,128)(2,1)S(1)}, bf16[1024,384]{1,0:T(8,128)(2,1)}, u32[]{:S(2)}) copy-start(bf16[1024,384]{1,0:T(8,128)(2,1)} %copy-done.5) | copy-start | bytes 2359300
  159.1 19.5 %copy-start.40 = (f32[24,1024]{1,0:T(8,128)S(1)}, f32[24,1024]{1,0:T(8,128)}, u32[]{:S(2)}) copy-start(f32[24,1024]{1,0:T(8,128)} %copy-done.39) | copy-start | bytes 294916
  208.1 9.3 %collective-permute-start.16 = (bf16[1024,1024]{1,0:T(8,128)(2,1)}, bf16[1024,1024]{1,0:T(8,128)(2,1)}, u32[]{:S(2)}, u32[]{:S(2)}) collective-permute-start(bf16[1024,1024]{1,0:T(8,128)(2,1)} %back_half.2), channel_id=1, source_target_pairs={{0,8},{1,9},{2,10},{3,11},{4,12},{5,13},{6,14},{7,15},{8,0},{9,1},... | collective-permute-start | bytes 6291464 | tf_op jit(solution)/shard_map/ppermute | solution.py:105
  208.1 47.7 %all-to-all-start.3 = ((bf16[64,16,512]{2,1,0:T(8,128)(2,1)}), bf16[64,16,512]{2,1,0:T(8,128)(2,1)}, u32[]{:S(2)}, u32[]{:S(2)}) async-start(bf16[64,16,512]{2,1,0:T(8,128)(2,1)} %bitcast.18), calls=%async_computation.3 | async-start | bytes 2097152 | tf_op jit(solution)/shard_map/all_to_all | solution.py:109
  217.3 14.4 %copy-start.44 = (s32[4]{0:T(128)S(1)}, s32[4]{0:T(128)}, u32[]{:S(2)}) copy-start(s32[4]{0:T(128)} %copy-done.43) | copy-start | bytes 52
  220.3 33.6 %copy-start.26 = (bf16[256,1024]{1,0:T(8,128)(2,1)S(1)}, bf16[256,1024]{1,0:T(8,128)(2,1)}, u32[]{:S(2)}) copy-start(bf16[256,1024]{1,0:T(8,128)(2,1)} %x_ref.3) | copy-start | bytes 1572868
  220.3 15.3 %collective-permute-start.17 = (bf16[256,1024]{1,0:T(8,128)(2,1)S(1)}, bf16[256,1024]{1,0:T(8,128)(2,1)S(1)}, u32[]{:S(2)}, u32[]{:S(2)}) collective-permute-start(bf16[256,1024]{1,0:T(8,128)(2,1)S(1)} %get-tuple-element.143), channel_id=1, source_target_pairs={{0,0},{1,1},{2,2},{3,3},{8,4},{9,5},{10,6},{11,7},{4,8},{5,9},{6,1... | collective-permute-start | bytes 1572872 | tf_op jit(solution)/shard_map/ppermute | solution.py:101
  225.6 14.7 %collective-permute-start.18 = (bf16[256,1024]{1,0:T(8,128)(2,1)S(1)}, bf16[256,1024]{1,0:T(8,128)(2,1)S(1)}, u32[]{:S(2)}, u32[]{:S(2)}) collective-permute-start(bf16[256,1024]{1,0:T(8,128)(2,1)S(1)} %get-tuple-element.144), channel_id=1, source_target_pairs={{1,0},{2,1},{3,2},{0,3},{9,4},{10,5},{11,6},{8,7},{5,8},{6,9},{7,1... | collective-permute-start | bytes 1572872 | tf_op jit(solution)/shard_map/ppermute | solution.py:101
  227.9 21.4 %collective-permute-start.19 = (bf16[256,1024]{1,0:T(8,128)(2,1)S(1)}, bf16[256,1024]{1,0:T(8,128)(2,1)S(1)}, u32[]{:S(2)}, u32[]{:S(2)}) collective-permute-start(bf16[256,1024]{1,0:T(8,128)(2,1)S(1)} %get-tuple-element.145), channel_id=1, source_target_pairs={{2,0},{3,1},{0,2},{1,3},{10,4},{11,5},{8,6},{9,7},{6,8},{7,9},{4,1... | collective-permute-start | bytes 1572872 | tf_op jit(solution)/shard_map/ppermute | solution.py:101
  231.4 22.5 %collective-permute-start.20 = (bf16[256,1024]{1,0:T(8,128)(2,1)S(1)}, bf16[256,1024]{1,0:T(8,128)(2,1)S(1)}, u32[]{:S(2)}, u32[]{:S(2)}) collective-permute-start(bf16[256,1024]{1,0:T(8,128)(2,1)S(1)} %get-tuple-element.146), channel_id=1, source_target_pairs={{3,0},{0,1},{1,2},{2,3},{11,4},{8,5},{9,6},{10,7},{7,8},{4,9},{5,1... | collective-permute-start | bytes 1572872 | tf_op jit(solution)/shard_map/ppermute | solution.py:101
  234.0 21.8 %collective-permute-start.21 = (bf16[16,1024]{1,0:T(8,128)(2,1)S(1)}, bf16[16,1024]{1,0:T(8,128)(2,1)S(1)}, u32[]{:S(2)}, u32[]{:S(2)}) collective-permute-start(bf16[16,1024]{1,0:T(8,128)(2,1)S(1)} %get-tuple-element.149), channel_id=1, source_target_pairs={{0,1},{1,2},{2,3},{3,0},{4,5},{5,6},{6,7},{7,4},{8,9},{9,10},{10,1... | collective-permute-start | bytes 98312 | tf_op jit(solution)/shard_map/ppermute | solution.py:988
  235.6 20.2 %collective-permute-start.22 = (bf16[16,1024]{1,0:T(8,128)(2,1)S(1)}, bf16[16,1024]{1,0:T(8,128)(2,1)S(1)}, u32[]{:S(2)}, u32[]{:S(2)}) collective-permute-start(bf16[16,1024]{1,0:T(8,128)(2,1)S(1)} %get-tuple-element.150), channel_id=1, source_target_pairs={{0,2},{1,3},{2,0},{3,1},{4,6},{5,7},{6,4},{7,5},{8,10},{9,11},{10,... | collective-permute-start | bytes 98312 | tf_op jit(solution)/shard_map/ppermute | solution.py:988
  240.2 15.5 %collective-permute-start.23 = (bf16[16,1024]{1,0:T(8,128)(2,1)S(1)}, bf16[16,1024]{1,0:T(8,128)(2,1)S(1)}, u32[]{:S(2)}, u32[]{:S(2)}) collective-permute-start(bf16[16,1024]{1,0:T(8,128)(2,1)S(1)} %get-tuple-element.151), channel_id=1, source_target_pairs={{0,3},{1,0},{2,1},{3,2},{4,7},{5,4},{6,5},{7,6},{8,11},{9,8},{10,9... | collective-permute-start | bytes 98312 | tf_op jit(solution)/shard_map/ppermute | solution.py:988
  257.2 28.0 %copy-start.32 = (bf16[256,1024]{1,0:T(8,128)(2,1)S(1)}, bf16[256,1024]{1,0:T(8,128)(2,1)}, u32[]{:S(2)}) copy-start(bf16[256,1024]{1,0:T(8,128)(2,1)} %copy-done.31) | copy-start | bytes 1572868
  257.3 28.0 %copy-start.34 = (bf16[256,1024]{1,0:T(8,128)(2,1)S(1)}, bf16[256,1024]{1,0:T(8,128)(2,1)}, u32[]{:S(2)}) copy-start(bf16[256,1024]{1,0:T(8,128)(2,1)} %copy-done.33) | copy-start | bytes 1572868
  257.3 28.0 %copy-start.36 = (bf16[256,1024]{1,0:T(8,128)(2,1)S(1)}, bf16[256,1024]{1,0:T(8,128)(2,1)}, u32[]{:S(2)}) copy-start(bf16[256,1024]{1,0:T(8,128)(2,1)} %copy-done.35) | copy-start | bytes 1572868
  257.3 28.0 %copy-start.38 = (bf16[256,1024]{1,0:T(8,128)(2,1)S(1)}, bf16[256,1024]{1,0:T(8,128)(2,1)}, u32[]{:S(2)}) copy-start(bf16[256,1024]{1,0:T(8,128)(2,1)} %copy-done.37) | copy-start | bytes 1572868
  284.4 4.1 %collective-permute-start.24 = (bf16[128,6784]{1,0:T(8,128)(2,1)S(1)}, bf16[128,6784]{1,0:T(8,128)(2,1)S(1)}, u32[]{:S(2)}, u32[]{:S(2)}) collective-permute-start(bf16[128,6784]{1,0:T(8,128)(2,1)S(1)} %bitcast.16), channel_id=1, source_target_pairs={{0,8},{1,9},{2,10},{3,11},{4,12},{5,13},{6,14},{7,15},{8,0},{9,1},... | collective-permute-start | bytes 5210120 | tf_op jit(solution)/shard_map/ppermute | solution.py:105
  (46 other events, 126.8 us)
